TPU v7x, 32 devices: a whole 2x2x4 slice. The times are simulated.
32 devices in a mesh: tok: 4 (over z), con: 4 (over x, core), out: 2 (over y).
Axes of the slice: x: 2, y: 2, z: 4, core: 2. Of those that a mesh axis runs over, the one named last changes fastest.
Arguments:
- tokens: bfloat16 [1024, 10240], P('tok', 'con'), may hold values from -6 to 6
- out_grad: bfloat16 [1024, 10240], P('tok', 'con'), may hold values from -3 to 3
- weight_in: bfloat16 [10240, 20480], P('con', ('tok', 'out')), may hold values from -0.0625 to 0.0625
- weight_out: bfloat16 [20480, 10240], P(('tok', 'out'), 'con'), may hold values from -0.0390625 to 0.0390625
Outputs:
- input_grad: bfloat16 [1024, 10240], P(('tok', 'out'), 'con')
- first_grad: float32 [10240, 20480], P('con', ('tok', 'out'))
- second_grad: float32 [20480, 10240], P(('tok', 'out'), 'con')
All inputs are finite; a program needn't handle non-finite values.
Results may differ from a plain program's by a relative error of at most 0.0049.
Values may be sent and summed in bfloat16 or wider, within the bound.
A program may use at most 192 MiB of HBM per device.

v0:
```python
import jax
import jax.numpy as jnp
from jax import lax
from jax.sharding import PartitionSpec as P


def gelu_parts(pre, act_grad):
    cdf = 0.5 * (1.0 + jax.scipy.special.erf(pre * 0.7071067811865476))
    density = jnp.exp(-0.5 * pre * pre) * 0.3989422804014327
    activ = (pre * cdf).astype(jnp.bfloat16)
    pre_grad = (act_grad * (cdf + pre * density)).astype(jnp.bfloat16)
    return (activ, pre_grad)


def per_device(tokens, out_grad, weight_in, weight_out):
    gathered_tok, gathered_grad = (
        lax.all_gather(tokens, "tok", axis=0, tiled=True),
        lax.all_gather(out_grad, "tok", axis=0, tiled=True),
    )
    pre_part = jnp.dot(gathered_tok, weight_in, preferred_element_type=jnp.float32)
    grad_part = lax.dot_general(
        gathered_grad, weight_out, (((1,), (1,)), ((), ())), preferred_element_type=jnp.float32
    )
    pre_share, grad_share = (
        lax.psum_scatter(pre_part, "con", scatter_dimension=0, tiled=True),
        lax.psum_scatter(grad_part, "con", scatter_dimension=0, tiled=True),
    )
    activ_share, pre_grad_share = gelu_parts(pre_share, grad_share)
    activ, pre_grad = (
        lax.all_gather(activ_share, "con", axis=0, tiled=True),
        lax.all_gather(pre_grad_share, "con", axis=0, tiled=True),
    )
    first_grad = lax.dot_general(
        gathered_tok, pre_grad, (((0,), (0,)), ((), ())), preferred_element_type=jnp.float32
    )
    second_grad = lax.dot_general(
        activ, gathered_grad, (((0,), (0,)), ((), ())), preferred_element_type=jnp.float32
    )
    summed = lax.psum_scatter(
        lax.dot_general(
            pre_grad, weight_in, (((1,), (1,)), ((), ())), preferred_element_type=jnp.float32
        ),
        ("tok", "out"),
        scatter_dimension=0,
        tiled=True,
    )
    return (summed.astype(jnp.bfloat16), first_grad, second_grad)


def solution(mesh):
    placed = (P("tok", "con"), P("tok", "con"), P("con", ("tok", "out")), P(("tok", "out"), "con"))
    return jax.shard_map(
        per_device,
        mesh=mesh,
        in_specs=placed,
        out_specs=(P(("tok", "out"), "con"), P("con", ("tok", "out")), P(("tok", "out"), "con")),
        check_vma=False,
    )
```

profile of v0, /device:TPU:0, one launch (start us, length us, event | category | flops | bytes accessed | tf_op | source)
XLA Modules:
  0.0 660.9 jit_solution(17489417421836680662)
XLA Ops:
  7.2 0.0 all-gather.5.cloned.1.call-start
  7.2 0.7 all-gather.5.cloned.1.call-update
  7.9 0.0 all-gather.7.cloned.1.call-start
  7.9 0.7 all-gather.7.cloned.1.call-update
  8.6 0.0 reduce-scatter.4.cloned.1.call-start
  8.7 101.7 %all-gather.5.cloned.1.call-done = bf16[1024,2560]{1,0:T(8,128)(2,1)} async-done(((bf16[256,2560]{1,0:T(8,128)(2,1)}), bf16[1024,2560]{1,0:T(8,128)(2,1)}) %all-gather.5.cloned.1.call-update) | async-done | bytes 5242896 | tf_op jit(solution)/shard_map/all_gather | solution.py:18
  110.4 20.6 %fusion.6 = f32[1024,2560]{1,0:T(8,128)} fusion(bf16[1024,2560]{1,0:T(8,128)(2,1)} %all-gather.5.cloned.1.call-done, bf16[2560,2560]{1,0:T(8,128)(2,1)} %param.7), kind=kOutput, calls=%fused_computation.10 | convolution fusion | flops 13421772800 | bytes 28835840 | tf_op jit(solution)/shard_map/dot_general | solution.py:21
  131.0 0.0 reduce-scatter.4.cloned.1.call-update
  131.0 0.0 reduce-scatter.6.cloned.1.call-start
  131.1 77.3 %all-gather.7.cloned.1.call-done = bf16[1024,2560]{1,0:T(8,128)(2,1)} async-done(((bf16[256,2560]{1,0:T(8,128)(2,1)}), bf16[1024,2560]{1,0:T(8,128)(2,1)}) %all-gather.7.cloned.1.call-update) | async-done | bytes 5242896 | tf_op jit(solution)/shard_map/all_gather | solution.py:17
  208.4 20.6 %fusion.7 = f32[1024,2560]{1,0:T(8,128)} fusion(bf16[1024,2560]{1,0:T(8,128)(2,1)} %all-gather.7.cloned.1.call-done, bf16[2560,2560]{1,0:T(8,128)(2,1)} %param.6), kind=kOutput, calls=%fused_computation.11 | convolution fusion | flops 13421772800 | bytes 28835840 | tf_op jit(solution)/shard_map/dot_general | solution.py:20
  229.0 0.0 reduce-scatter.6.cloned.1.call-update
  229.0 0.0 all-gather.9.cloned.1.call-start
  229.1 66.2 %reduce-scatter.4.cloned.1.call-done = f32[256,2560]{1,0:T(8,128)} async-done(((f32[1024,2560]{1,0:T(8,128)}), f32[256,2560]{1,0:T(8,128)}) %reduce-scatter.4.cloned.1.call-update) | async-done | bytes 2621456 | tf_op jit(solution)/shard_map/reduce_scatter | solution.py:26
  295.3 88.4 %reduce-scatter.6.cloned.1.call-done = f32[256,2560]{1,0:T(8,128)} async-done(((f32[1024,2560]{1,0:T(8,128)}), f32[256,2560]{1,0:T(8,128)}) %reduce-scatter.6.cloned.1.call-update) | async-done | bytes 2621456 | tf_op jit(solution)/shard_map/reduce_scatter | solution.py:25
  383.7 4.1 multiply_convert_fusion
  387.8 0.0 all-gather.9.cloned.1.call-update
  387.8 0.0 all-gather.11.cloned.1.call-start
  387.9 0.5 all-gather.11.cloned.1.call-update
  388.4 0.2 reduce-scatter.8.cloned.1.call-start
  388.6 39.8 %all-gather.9.cloned.1.call-done = bf16[1024,2560]{1,0:T(8,128)(2,1)} async-done(((bf16[256,2560]{1,0:T(8,128)(2,1)}), bf16[1024,2560]{1,0:T(8,128)(2,1)}) %all-gather.9.cloned.1.call-update) | async-done | bytes 5242896 | tf_op jit(solution)/shard_map/all_gather | solution.py:31
  428.4 20.7 %fusion.8 = f32[1024,2560]{1,0:T(8,128)} fusion(bf16[1024,2560]{1,0:T(8,128)(2,1)} %all-gather.9.cloned.1.call-done, bf16[2560,2560]{1,0:T(8,128)(2,1)} %param.6), kind=kOutput, calls=%fused_computation.12 | convolution fusion | flops 13421772800 | bytes 28835840 | tf_op jit(solution)/shard_map/dot_general | solution.py:40
  449.1 0.0 reduce-scatter.8.cloned.1.call-update
  449.2 22.3 %convolution_bitcast_fusion = f32[2560,2560]{0,1:T(8,128)} fusion(bf16[1024,2560]{1,0:T(8,128)(2,1)} %all-gather.9.cloned.1.call-done, bf16[1024,2560]{1,0:T(8,128)(2,1)} %all-gather.7.cloned.1.call-done), kind=kOutput, calls=%fused_computation | convolution fusion | flops 13421772800 | bytes 36700160 | tf_op jit(solution)/shard_map/dot_general | solution.py:33
  471.5 27.4 %copy.7 = f32[2560,2560]{1,0:T(8,128)} copy(f32[2560,2560]{0,1:T(8,128)} %convolution_bitcast_fusion) | data formatting | bytes 52428800
  498.9 0.0 all-gather.11.cloned.1.call-done
  498.9 22.4 %fusion.9 = f32[2560,2560]{1,0:T(8,128)} fusion(bf16[1024,2560]{1,0:T(8,128)(2,1)} %all-gather.11.cloned.1.call-done, bf16[1024,2560]{1,0:T(8,128)(2,1)} %all-gather.5.cloned.1.call-done), kind=kOutput, calls=%fused_computation.13 | convolution fusion | flops 13421772800 | bytes 36700160 | tf_op jit(solution)/shard_map/dot_general | solution.py:36
  521.2 130.6 %reduce-scatter.8.cloned.1.call-done = f32[128,2560]{1,0:T(8,128)} async-done(((f32[1024,2560]{1,0:T(8,128)}), f32[128,2560]{1,0:T(8,128)}) %reduce-scatter.8.cloned.1.call-update) | async-done | bytes 1310736 | tf_op jit(solution)/shard_map/reduce_scatter | solution.py:39
  651.9 2.2 convert_element_type.10
Async XLA Ops:
  7.2 103.2 %all-gather.5.cloned.1.call-start = ((), (), s32[]{:S(2)}) async-start(), calls=%async_computation.3 | async-start | bytes 6553600 | tf_op jit(solution)/shard_map/all_gather | solution.py:18
  7.9 200.5 %all-gather.7.cloned.1.call-start = ((), (), s32[]{:S(2)}) async-start(), calls=%async_computation.5 | async-start | bytes 6553600 | tf_op jit(solution)/shard_map/all_gather | solution.py:17
  8.6 286.6 %reduce-scatter.4.cloned.1.call-start = ((), (), s32[]{:S(2)}) async-start(), calls=%async_computation.4 | async-start | bytes 13107200 | tf_op jit(solution)/shard_map/reduce_scatter | solution.py:26
  131.0 252.6 %reduce-scatter.6.cloned.1.call-start = ((), (), s32[]{:S(2)}) async-start(), calls=%async_computation.6 | async-start | bytes 13107200 | tf_op jit(solution)/shard_map/reduce_scatter | solution.py:25
  229.0 199.4 %all-gather.9.cloned.1.call-start = ((), (), s32[]{:S(2)}) async-start(), calls=%async_computation.7 | async-start | bytes 6553600 | tf_op jit(solution)/shard_map/all_gather | solution.py:31
  387.8 111.0 %all-gather.11.cloned.1.call-start = ((), (), s32[]{:S(2)}) async-start(), calls=%async_computation.9 | async-start | bytes 6553600 | tf_op jit(solution)/shard_map/all_gather | solution.py:30
  388.4 263.4 %reduce-scatter.8.cloned.1.call-start = ((), (), s32[]{:S(2)}) async-start(), calls=%async_computation.8 | async-start | bytes 11796480 | tf_op jit(solution)/shard_map/reduce_scatter | solution.py:39
Sparse Core Ops, SparseCore 0:
  9.6 100.7 all-gather.4
  111.9 96.4 all-gather.6
  211.6 83.6 reduce-scatter.3
  298.3 85.2 reduce-scatter.5
  388.0 40.4 all-gather.8
  429.8 40.4 all-gather.10
  473.9 177.9 reduce-scatter.7
where the time goes:
time: 662 us; the launch traced here: 661 us
  waiting for transfers between devices  506 us (76%)
  matrix products  107 us (16%)
  local copies, waits for them, and re-layouts  27.4 us (4%)
  between operations  14.1 us (2%)
    reduce_scatter x1, waiting for transfers between devices, per_device(): lax.psum_scatter(lax.dot_general(pre_grad, weight_in, (((1,), (1,)), ((),...  131 us
    all_gather x1, waiting for transfers between devices, per_device(): lax.all_gather(out_grad, 'tok', axis=0, tiled=True)  102 us
    reduce_scatter x1, waiting for transfers between devices, per_device(): lax.psum_scatter(pre_part, 'con', scatter_dimension=0, tiled=True)  88.4 us
    all_gather x1, waiting for transfers between devices, per_device(): lax.all_gather(tokens, 'tok', axis=0, tiled=True)  77.3 us
    reduce_scatter x1, waiting for transfers between devices, per_device(): lax.psum_scatter(grad_part, 'con', scatter_dimension=0, tiled=True)  66.2 us
    all_gather x1, waiting for transfers between devices, per_device(): lax.all_gather(pre_grad_share, 'con', axis=0, tiled=True)  39.8 us
    unnamed x1, local copies, waits for them, and re-layouts  27.4 us
    dot_general x1, matrix products, per_device(): lax.dot_general(activ, gathered_grad, (((0,), (0,)), ((), ())), preferred...  22.4 us
  transfers between devices with their start and end apart: 7, of which 6 were waited for; matrix products, arithmetic and copies ran while one was open for 20% of the time, Pallas kernels for 0%

commit v1 on v0

v1 whole, which is shorter than its diff:
```python
import functools

import jax
import jax.numpy as jnp
from jax import lax
from jax.experimental import pallas as pl
from jax.experimental.pallas import tpu as pltpu
from jax.sharding import PartitionSpec as P


def gelu_parts(pre, act_grad):
    cdf = 0.5 * (1.0 + jax.scipy.special.erf(pre * 0.7071067811865476))
    density = jnp.exp(-0.5 * pre * pre) * 0.3989422804014327
    activ = (pre * cdf).astype(jnp.bfloat16)
    pre_grad = (act_grad * (cdf + pre * density)).astype(jnp.bfloat16)
    return (activ, pre_grad)


def grad_kernel(chunks, width, *refs):
    left, right, out = refs[:chunks], refs[chunks : 2 * chunks], refs[-1]
    total = out.shape[1]
    for start in range(0, total, width):
        acc = None
        for a, b in zip(left, right):
            term = lax.dot_general(
                a[...],
                b[:, start : start + width],
                (((0,), (0,)), ((), ())),
                preferred_element_type=jnp.float32,
            )
            acc = term if acc is None else acc + term
        out[:, start : start + width] = acc


def summed_outer(left, left_from, left_width, right, right_block, right_width):
    chunks, rows = len(left), left[0].shape[0]
    high = 256 if left_width % 256 == 0 else 128
    width = 512 if right_width % 512 == 0 else 128
    first = left_from // high
    return pl.pallas_call(
        functools.partial(grad_kernel, chunks, width),
        grid=(left_width // high,),
        in_specs=[pl.BlockSpec((rows, high), lambda i: (0, first + i))] * chunks
        + [pl.BlockSpec((rows, right_width), lambda i: (0, right_block))] * chunks,
        out_specs=pl.BlockSpec((high, right_width), lambda i: (i, 0)),
        out_shape=jax.ShapeDtypeStruct((left_width, right_width), jnp.float32),
        compiler_params=pltpu.CompilerParams(
            dimension_semantics=("arbitrary",), vmem_limit_bytes=32 * 1024 * 1024
        ),
        cost_estimate=pl.CostEstimate(
            flops=2 * chunks * rows * left_width * right_width,
            bytes_accessed=4 * left_width * right_width
            + 2 * chunks * rows * (left_width + right_width),
            transcendentals=0,
        ),
    )(*left, *right)


def per_device(T, C, O, tokens, out_grad, weight_in, weight_out):
    bf16, f32 = jnp.bfloat16, jnp.float32
    o, c = lax.axis_index("out"), lax.axis_index("con")
    inner = 2 if C % 2 == 0 else 1
    outer = C // inner
    ci, co = c % inner, c // inner

    def shift(a, axis, size, by):
        return lax.ppermute(a, axis, [(i, (i + by) % size) for i in range(size)])

    def shift_inner(a, by):
        return lax.ppermute(
            a, "con", [(i, i // inner * inner + (i % inner + by) % inner) for i in range(C)]
        )

    def shift_outer(a, by):
        return lax.ppermute(
            a, "con", [(i, (i // inner + by) % outer * inner + i % inner) for i in range(C)]
        )

    shard = tokens.shape[0]
    rows = shard // O
    hidden = weight_in.shape[1]

    def part(a, k):
        return lax.dynamic_slice_in_dim(a, (o - k) % O * rows, rows, 0)

    def whole_shard(own):
        return jnp.concatenate([own] + [shift(own, "out", O, k) for k in range(1, O)], axis=0)

    tok_part, grad_part = part(tokens, 0), part(out_grad, 0)
    toks = [jnp.concatenate([part(tokens, k) for k in range(O)], axis=0)]
    grads = [jnp.concatenate([part(out_grad, k) for k in range(O)], axis=0)]
    for _ in range(1, T):
        tok_part = shift(tok_part, "tok", T, 1)
        grad_part = shift(grad_part, "tok", T, 1)
        toks.append(whole_shard(tok_part))
        grads.append(whole_shard(grad_part))

    def con_sum(pre, grad):
        pre = pre.reshape(outer, inner, shard // C, hidden)
        grad = grad.reshape(outer, inner, shard // C, hidden)

        def pick(a, axis, at):
            return lax.dynamic_index_in_dim(a, at, axis, keepdims=False)

        kept = [pick(pre, 1, ci), pick(grad, 1, ci)]
        for k in range(1, inner):
            to = (ci - k) % inner
            kept[0] = kept[0] + shift_inner(pick(pre, 1, to), -k)
            kept[1] = kept[1] + shift_inner(pick(grad, 1, to), -k)
        held = [pick(kept[0], 0, co), pick(kept[1], 0, co)]
        for k in range(1, outer):
            to = (co - k) % outer
            sent = jnp.concatenate([pick(kept[0], 0, to), pick(kept[1], 0, to)], axis=1)
            got = shift_outer(sent.astype(bf16), -k).astype(f32)
            held = [held[0] + got[:, :hidden], held[1] + got[:, hidden:]]
        return held

    both, result = [], None
    for k in range(T):
        pre = jnp.dot(toks[k], weight_in, preferred_element_type=f32)
        grad = lax.dot_general(
            grads[k], weight_out, (((1,), (1,)), ((), ())), preferred_element_type=f32
        )
        share = jnp.concatenate(gelu_parts(*con_sum(pre, grad)), axis=1)
        chunk = lax.all_gather(share, "con", axis=0, tiled=True)
        both.append(chunk)
        back = lax.dot_general(
            chunk[:, hidden:], weight_in, (((1,), (1,)), ((), ())), preferred_element_type=f32
        )
        total = back[:rows]
        for j in range(1, O):
            sent = back[j * rows : (j + 1) * rows].astype(bf16)
            total = total + shift(sent, "out", O, -j).astype(f32)
        if k:
            total = shift(total.astype(bf16), "tok", T, -k).astype(f32)
        result = total if result is None else result + total

    width = tokens.shape[1]
    first_grad = summed_outer(toks, 0, width, both, 1, hidden)
    second_grad = summed_outer(both, 0, hidden, grads, 0, width)
    return (result.astype(bf16), first_grad, second_grad)


def solution(mesh):
    placed = (P("tok", "con"), P("tok", "con"), P("con", ("tok", "out")), P(("tok", "out"), "con"))
    sizes = [mesh.shape[axis] for axis in ("tok", "con", "out")]
    return jax.shard_map(
        functools.partial(per_device, *sizes),
        mesh=mesh,
        in_specs=placed,
        out_specs=(P(("tok", "out"), "con"), P("con", ("tok", "out")), P(("tok", "out"), "con")),
        check_vma=False,
    )
```

time: 662 us -> 325 us (0.49)
  waiting for transfers between devices: 506 us -> 88.3 us
  Pallas kernels: 0 us -> 35.9 us
  starting transfers between devices: 0.46 us -> 36 us
  matrix products: 107 us -> 85.3 us
  other arithmetic: 6.37 us -> 24 us
  local copies, waits for them, and re-layouts: 27.4 us -> 39.9 us
    reduce_scatter x3 -> x0, waiting for transfers between devices: 285 us -> none  [the longest x1 131 us: per_device(): lax.psum_scatter(lax.dot_general(pre_grad, weight_in, (((1,), (1,)), ((),...]
    all_gather x4, waiting for transfers between devices: 219 us -> 0.03 us  [per_device(): chunk = lax.all_gather(share, 'con', axis=0, tiled=True)]
    ppermute x0 -> x31, waiting for transfers between devices: none -> 88.2 us  [the longest x19 59.8 us: shift(): return lax.ppermute(a, axis, [(i, (i + by) % size) for i in range(size)])]
    pallas_call x0 -> x2, Pallas kernels: none -> 35.9 us  [summed_outer(): pl.pallas_call(functools.partial(grad_kernel, chunks, width), grid=(left_...]
    ppermute x0 -> x31, starting transfers between devices: none -> 35.6 us  [the longest x19 31.1 us: shift(): return lax.ppermute(a, axis, [(i, (i + by) % size) for i in range(size)])]
    dot_general x5 -> x12, matrix products: 107 us -> 85.3 us  [the longest x4 29.1 us: per_device(): lax.dot_general(chunk[:, hidden:], weight_in, (((1,), (1,)), ((), ())), p...]
    add x0 -> x8, other arithmetic: none -> 11.4 us  [the longest x4 6.77 us: con_sum(): kept[0] = kept[0] + shift_inner(pick(pre, 1, to), -k)]
    squeeze x0 -> x16, local copies, waits for them, and re-layouts: none -> 10.3 us  [pick(): return lax.dynamic_index_in_dim(a, at, axis, keepdims=False)]
  transfers between devices with their start and end apart: 7 -> 35, of which waited for: 6 -> 13; matrix products, arithmetic and copies ran while one was open for 20% -> 39% of each run, Pallas kernels for 0% -> 11%
where the time goes in v1:
time: 325 us; the launch traced here: 324 us
  waiting for transfers between devices  88.3 us (27%)
  matrix products  85.3 us (26%)
  local copies, waits for them, and re-layouts  39.9 us (12%)
  starting transfers between devices  36 us (11%)
  Pallas kernels  35.9 us (11%)
  other arithmetic  24 us (7%)
  between operations  14.6 us (4%)
    ppermute x19, waiting for transfers between devices, shift(): return lax.ppermute(a, axis, [(i, (i + by) % size) for i in range(size)])  59.8 us
    pallas_call x2, Pallas kernels, summed_outer(): pl.pallas_call(functools.partial(grad_kernel, chunks, width), grid=(left_...  35.9 us
    ppermute x19, starting transfers between devices, shift(): return lax.ppermute(a, axis, [(i, (i + by) % size) for i in range(size)])  31.1 us
    dot_general x4, matrix products, per_device(): lax.dot_general(chunk[:, hidden:], weight_in, (((1,), (1,)), ((), ())), p...  29.1 us
    ppermute x4, waiting for transfers between devices, shift_outer(): lax.ppermute(a, 'con', [(i, (i // inner + by) % outer * inner + i % inner...  28.4 us
    dot_general x4, matrix products, per_device(): lax.dot_general(grads[k], weight_out, (((1,), (1,)), ((), ())), preferred...  28.2 us
    dot_general x4, matrix products, per_device(): pre = jnp.dot(toks[k], weight_in, preferred_element_type=f32)  27.9 us
    unnamed x90, local copies, waits for them, and re-layouts  24.7 us
  transfers between devices with their start and end apart: 35, of which 13 were waited for; matrix products, arithmetic and copies ran while one was open for 39% of the time, Pallas kernels for 11%

profile of v1, /device:TPU:0, one launch (start us, length us, event | category | flops | bytes accessed | tf_op | source)
XLA Modules:
  0.0 323.9 jit_solution(11196488431127978377)
XLA Ops:
  8.7 3.1 collective-permute-start.4
  13.0 1.6 collective-permute-start.7
  14.6 6.6 %fusion.48 = f32[256,2560]{1,0:T(8,128)S(1)} fusion(bf16[2560,2560]{1,0:T(8,128)(2,1)} %param.6, bf16[128,2560]{1,0:T(8,128)(2,1)S(1)} %get-tuple-element.12, bf16[128,2560]{1,0:T(8,128)(2,1)S(1)} %get-tuple-element.11), kind=kOutput, calls=%fused_computation.126 | convolution fusion | flops 3358064640 | bytes 17039360 | tf_op jit(solution)/shard_map/dot_general | solution.py:120
  23.1 6.8 %fusion.47 = f32[256,2560]{1,0:T(8,128)S(1)} fusion(bf16[2560,2560]{1,0:T(8,128)(2,1)} %param.7, bf16[128,2560]{1,0:T(8,128)(2,1)S(1)} %copy-done.33, bf16[128,2560]{1,0:T(8,128)(2,1)} %get-tuple-element.13), kind=kOutput, calls=%fused_computation.125 | convolution fusion | flops 3358064640 | bytes 17039360 | tf_op jit(solution)/shard_map/dot_general | solution.py:121
  33.2 1.6 collective-permute-start.13
  34.8 8.8 %collective-permute-done.7 = bf16[128,2560]{1,0:T(8,128)(2,1)} collective-permute-done((bf16[128,2560]{1,0:T(8,128)(2,1)}, bf16[128,2560]{1,0:T(8,128)(2,1)}, u32[]{:S(2)}, u32[]{:S(2)}) %collective-permute-start.7) | collective-permute-done | bytes 655392 | tf_op jit(solution)/shard_map/ppermute | solution.py:67
  43.6 1.8 collective-permute-start.8
  47.6 1.9 collective-permute-done.5
  49.5 1.6 collective-permute-start.16
  51.1 7.1 %fusion.49 = f32[256,2560]{1,0:T(8,128)S(1)} fusion(bf16[256,2560]{1,0:T(8,128)(2,1)S(1)} %constant_dynamic-update-slice_fusion.refs_1_, bf16[2560,2560]{1,0:T(8,128)(2,1)} %param.6), kind=kOutput, calls=%fused_computation.127 | convolution fusion | flops 3355443200 | bytes 17039360 | tf_op jit(solution)/shard_map/dot_general | solution.py:120
  60.2 2.4 collective-permute-done.8
  62.6 7.1 %fusion.50 = f32[256,2560]{1,0:T(8,128)S(1)} fusion(bf16[256,2560]{1,0:T(8,128)(2,1)S(1)} %constant_dynamic-update-slice_fusion.2.refs_5_, bf16[2560,2560]{1,0:T(8,128)(2,1)} %param.7), kind=kOutput, calls=%fused_computation.128 | convolution fusion | flops 3355443200 | bytes 17039360 | tf_op jit(solution)/shard_map/dot_general | solution.py:121
  76.0 1.6 collective-permute-start.2
  81.9 13.5 %collective-permute-done.14 = bf16[128,2560]{1,0:T(8,128)(2,1)S(1)} collective-permute-done((bf16[128,2560]{1,0:T(8,128)(2,1)}, bf16[128,2560]{1,0:T(8,128)(2,1)S(1)}, u32[]{:S(2)}, u32[]{:S(2)}) %collective-permute-start.14) | collective-permute-done | bytes 655392 | tf_op jit(solution)/shard_map/ppermute | solution.py:67
  95.4 1.6 collective-permute-start.22
  97.0 7.1 %fusion.51 = f32[256,2560]{1,0:T(8,128)S(1)} fusion(bf16[256,2560]{1,0:T(8,128)(2,1)S(1)} %constant_dynamic-update-slice_fusion.4.refs_2_, bf16[2560,2560]{1,0:T(8,128)(2,1)} %param.6), kind=kOutput, calls=%fused_computation.129 | convolution fusion | flops 3355443200 | bytes 17039360 | tf_op jit(solution)/shard_map/dot_general | solution.py:120
  104.1 4.6 %collective-permute-done.17 = bf16[128,2560]{1,0:T(8,128)(2,1)S(1)} collective-permute-done((bf16[128,2560]{1,0:T(8,128)(2,1)}, bf16[128,2560]{1,0:T(8,128)(2,1)S(1)}, u32[]{:S(2)}, u32[]{:S(2)}) %collective-permute-start.17) | collective-permute-done | bytes 655392 | tf_op jit(solution)/shard_map/ppermute | solution.py:67
  108.7 1.6 collective-permute-start.25
  110.4 7.1 %fusion.52 = f32[256,2560]{1,0:T(8,128)S(1)} fusion(bf16[256,2560]{1,0:T(8,128)(2,1)S(1)} %constant_dynamic-update-slice_fusion.6.refs_6_, bf16[2560,2560]{1,0:T(8,128)(2,1)} %param.7), kind=kOutput, calls=%fused_computation.130 | convolution fusion | flops 3355443200 | bytes 17039360 | tf_op jit(solution)/shard_map/dot_general | solution.py:121
  123.3 3.7 %collective-permute-done.25 = bf16[128,2560]{1,0:T(8,128)(2,1)} collective-permute-done((bf16[128,2560]{1,0:T(8,128)(2,1)}, bf16[128,2560]{1,0:T(8,128)(2,1)}, u32[]{:S(2)}, u32[]{:S(2)}) %collective-permute-start.25) | collective-permute-done | bytes 655392 | tf_op jit(solution)/shard_map/ppermute | solution.py:67
  130.3 1.7 bitcast_add_fusion.5
  134.6 10.2 %collective-permute-done.23 = bf16[128,2560]{1,0:T(8,128)(2,1)S(1)} collective-permute-done((bf16[128,2560]{1,0:T(8,128)(2,1)}, bf16[128,2560]{1,0:T(8,128)(2,1)S(1)}, u32[]{:S(2)}, u32[]{:S(2)}) %collective-permute-start.23) | collective-permute-done | bytes 655392 | tf_op jit(solution)/shard_map/ppermute | solution.py:67
  144.9 7.1 %fusion.53 = f32[256,2560]{1,0:T(8,128)S(1)} fusion(bf16[256,2560]{1,0:T(8,128)(2,1)S(1)} %constant_dynamic-update-slice_fusion.8.refs_3_, bf16[2560,2560]{1,0:T(8,128)(2,1)} %param.6), kind=kOutput, calls=%fused_computation.131 | convolution fusion | flops 3355443200 | bytes 17039360 | tf_op jit(solution)/shard_map/dot_general | solution.py:120
  154.0 2.5 collective-permute-done.26
  158.9 2.0 bitcast_add_fusion.3
  162.1 7.1 %fusion.54 = f32[256,2560]{1,0:T(8,128)S(1)} fusion(bf16[256,2560]{1,0:T(8,128)(2,1)S(1)} %constant_dynamic-update-slice_fusion.10.refs_7_, bf16[2560,2560]{1,0:T(8,128)(2,1)} %param.7), kind=kOutput, calls=%fused_computation.132 | convolution fusion | flops 3355443200 | bytes 17039360 | tf_op jit(solution)/shard_map/dot_general | solution.py:121
  171.2 16.8 %collective-permute-done.19 = bf16[64,5120]{1,0:T(8,128)(2,1)S(1)} collective-permute-done((bf16[64,5120]{1,0:T(8,128)(2,1)S(1)}, bf16[64,5120]{1,0:T(8,128)(2,1)S(1)}, u32[]{:S(2)}, u32[]{:S(2)}) %collective-permute-start.19) | collective-permute-done | bytes 655392 | tf_op jit(solution)/shard_map/ppermute | solution.py:75
  190.0 1.6 bitcast_add_fusion.1
  192.2 1.6 bitcast_add_fusion
  196.1 10.7 %collective-permute-done.28 = bf16[64,5120]{1,0:T(8,128)(2,1)S(1)} collective-permute-done((bf16[64,5120]{1,0:T(8,128)(2,1)S(1)}, bf16[64,5120]{1,0:T(8,128)(2,1)S(1)}, u32[]{:S(2)}, u32[]{:S(2)}) %collective-permute-start.28) | collective-permute-done | bytes 655392 | tf_op jit(solution)/shard_map/ppermute | solution.py:75
  208.1 7.1 %fusion.13 = f32[256,2560]{1,0:T(8,128)S(1)} fusion(bf16[2560,2560]{1,0:T(8,128)(2,1)} %param.6, bf16[256,5120]{1,0:T(8,128)(2,1)} %all-gather.5.cloned.1.call-done.refs_4_.refs_0_), kind=kOutput, calls=%fused_computation.21 | convolution fusion | flops 3355443200 | bytes 17039360 | tf_op jit(solution)/shard_map/dot_general | solution.py:127
  217.7 1.5 collective-permute-start.3
  219.2 7.0 %fusion.7 = f32[256,2560]{1,0:T(8,128)S(1)} fusion(bf16[2560,2560]{1,0:T(8,128)(2,1)} %param.6, bf16[256,5120]{1,0:T(8,128)(2,1)} %all-gather.7.cloned.1.call-done.refs_5_.refs_1_), kind=kOutput, calls=%fused_computation.13 | convolution fusion | flops 3355443200 | bytes 17039360 | tf_op jit(solution)/shard_map/dot_general | solution.py:127
  229.2 7.8 %fusion.4 = f32[256,2560]{1,0:T(8,128)S(1)} fusion(bf16[2560,2560]{1,0:T(8,128)(2,1)} %param.6, bf16[256,5120]{1,0:T(8,128)(2,1)} %all-gather.9.cloned.1.call-done.refs_6_.refs_2_), kind=kOutput, calls=%fused_computation.8 | convolution fusion | flops 3355443200 | bytes 17039360 | tf_op jit(solution)/shard_map/dot_general | solution.py:127
  237.1 1.6 collective-permute-start.20
  238.7 7.9 %collective-permute-done.11 = bf16[128,2560]{1,0:T(8,128)(2,1)} collective-permute-done((bf16[128,2560]{1,0:T(8,128)(2,1)}, bf16[128,2560]{1,0:T(8,128)(2,1)}, u32[]{:S(2)}, u32[]{:S(2)}) %collective-permute-start.11) | collective-permute-done | bytes 655392 | tf_op jit(solution)/shard_map/ppermute | solution.py:67
  246.6 2.1 fusion.6
  248.7 3.4 %collective-permute-start.12 = (bf16[128,2560]{1,0:T(8,128)(2,1)}, bf16[128,2560]{1,0:T(8,128)(2,1)}, u32[]{:S(2)}, u32[]{:S(2)}) collective-permute-start(bf16[128,2560]{1,0:T(8,128)(2,1)} %fusion.6), channel_id=1, source_target_pairs={{0,24},{8,0},{16,8},{24,16},{1,25},{9,1},{17,9},{25,17},{2,26},{10... | collective-permute-start | bytes 1966088 | tf_op jit(solution)/shard_map/ppermute | solution.py:67
  252.1 4.4 %collective-permute-done.20 = bf16[128,2560]{1,0:T(8,128)(2,1)S(1)} collective-permute-done((bf16[128,2560]{1,0:T(8,128)(2,1)S(1)}, bf16[128,2560]{1,0:T(8,128)(2,1)S(1)}, u32[]{:S(2)}, u32[]{:S(2)}) %collective-permute-start.20) | collective-permute-done | bytes 655392 | tf_op jit(solution)/shard_map/ppermute | solution.py:67
  257.6 2.5 collective-permute-start.21
  260.1 7.2 %fusion.1 = f32[256,2560]{1,0:T(8,128)S(1)} fusion(bf16[2560,2560]{1,0:T(8,128)(2,1)} %param.6, bf16[256,5120]{1,0:T(8,128)(2,1)} %all-gather.11.cloned.1.call-done.refs_7_.refs_3_), kind=kOutput, calls=%fused_computation.3 | convolution fusion | flops 3355443200 | bytes 17039360 | tf_op jit(solution)/shard_map/dot_general | solution.py:127
  270.3 1.7 copy-done.12
  272.0 1.7 copy-done.14
  273.8 1.7 copy-done.16
  275.5 1.7 copy-done.17
  277.3 17.9 %shard_map.68 = f32[2560,2560]{1,0:T(8,128)} custom-call(bf16[256,5120]{1,0:T(8,128)(2,1)S(1)} %copy-done.12, bf16[256,5120]{1,0:T(8,128)(2,1)S(1)} %copy-done.14, bf16[256,5120]{1,0:T(8,128)(2,1)S(1)} %copy-done.16, bf16[256,5120]{1,0:T(8,128)(2,1)S(1)} %copy-done.17, bf16[256,2560]{1,0:T(8,128)(2,1)S(1)} %pad_maximum_fusion.1.refs_4_, ...), custom_call_target="tpu_custom_call" | custom-call | flops 13421772800 | bytes 36700160 | tf_op jit(solution)/shard_map/pallas_call | solution.py:40
  296.9 18.0 %shard_map.67 = f32[2560,2560]{1,0:T(8,128)} custom-call(bf16[256,2560]{1,0:T(8,128)(2,1)S(1)} %pad_maximum_fusion.refs_0_, bf16[256,2560]{1,0:T(8,128)(2,1)S(1)} %copy-done.9, bf16[256,2560]{1,0:T(8,128)(2,1)S(1)} %copy-done.11, bf16[256,2560]{1,0:T(8,128)(2,1)S(1)} %copy-done.3, bf16[256,5120]{1,0:T(8,128)(2,1)S(1)} %copy-done.13, ...), custom_call_target="tpu_custom_call" | custom-call | flops 13421772800 | bytes 36700160 | tf_op jit(solution)/shard_map/pallas_call | solution.py:40
  314.9 2.5 fusion.12
  (188 shorter events, 59.2 us)
Async XLA Ops:
  7.2 201.0 %all-gather.5.cloned.1.call-start = ((), (), s32[]{:S(2)}) async-start(), calls=%async_computation | async-start | bytes 3276800 | tf_op jit(solution)/shard_map/all_gather | solution.py:125
  8.7 22.9 %collective-permute-start.4 = (bf16[128,2560]{1,0:T(8,128)(2,1)S(1)}, bf16[128,2560]{1,0:T(8,128)(2,1)}, u32[]{:S(2)}, u32[]{:S(2)}) collective-permute-start(bf16[128,2560]{1,0:T(8,128)(2,1)S(1)} %get-tuple-element.11), channel_id=1, source_target_pairs={{0,8},{8,16},{16,24},{24,0},{1,9},{9,17},{17,25},{25,1},{2,10},{10... | collective-permute-start | bytes 1966088 | tf_op jit(solution)/shard_map/ppermute | solution.py:67
  13.0 30.6 %collective-permute-start.7 = (bf16[128,2560]{1,0:T(8,128)(2,1)}, bf16[128,2560]{1,0:T(8,128)(2,1)}, u32[]{:S(2)}, u32[]{:S(2)}) collective-permute-start(bf16[128,2560]{1,0:T(8,128)(2,1)} %get-tuple-element.13), channel_id=1, source_target_pairs={{0,8},{8,16},{16,24},{24,0},{1,9},{9,17},{17,25},{25,1},{2,10},{10... | collective-permute-start | bytes 1966088 | tf_op jit(solution)/shard_map/ppermute | solution.py:67
  23.1 48.7 %collective-permute-start = (f32[2,64,2560]{2,1,0:T(8,128)}, f32[2,64,2560]{2,1,0:T(8,128)}, u32[]{:S(2)}, u32[]{:S(2)}) collective-permute-start(f32[2,64,2560]{2,1,0:T(8,128)} %dynamic-slice_bitcast_fusion.7), channel_id=1, source_target_pairs={{0,2},{2,0},{4,6},{6,4},{1,3},{3,1},{5,7},{7,5},{8,10},{10,8},{12,... | collective-permute-start | bytes 3932168 | tf_op jit(solution)/shard_map/ppermute | solution.py:70
  31.1 43.3 %collective-permute-start.1 = (f32[2,64,2560]{2,1,0:T(8,128)}, f32[2,64,2560]{2,1,0:T(8,128)}, u32[]{:S(2)}, u32[]{:S(2)}) collective-permute-start(f32[2,64,2560]{2,1,0:T(8,128)} %dynamic-slice_bitcast_fusion.6), channel_id=1, source_target_pairs={{0,2},{2,0},{4,6},{6,4},{1,3},{3,1},{5,7},{7,5},{8,10},{10,8},{12,... | collective-permute-start | bytes 3932168 | tf_op jit(solution)/shard_map/ppermute | solution.py:70
  31.7 17.8 %collective-permute-start.5 = (bf16[128,2560]{1,0:T(8,128)(2,1)}, bf16[128,2560]{1,0:T(8,128)(2,1)S(1)}, u32[]{:S(2)}, u32[]{:S(2)}) collective-permute-start(bf16[128,2560]{1,0:T(8,128)(2,1)} %collective-permute-done.4), channel_id=1, source_target_pairs={{0,1},{1,0},{2,3},{3,2},{4,5},{5,4},{6,7},{7,6},{8,9},{9,8},{10,11... | collective-permute-start | bytes 1966088 | tf_op jit(solution)/shard_map/ppermute | solution.py:67
  33.2 44.4 %collective-permute-start.13 = (bf16[128,2560]{1,0:T(8,128)(2,1)}, bf16[128,2560]{1,0:T(8,128)(2,1)}, u32[]{:S(2)}, u32[]{:S(2)}) collective-permute-start(bf16[128,2560]{1,0:T(8,128)(2,1)} %collective-permute-done.4), channel_id=1, source_target_pairs={{0,8},{8,16},{16,24},{24,0},{1,9},{9,17},{17,25},{25,1},{2,10},{10... | collective-permute-start | bytes 1966088 | tf_op jit(solution)/shard_map/ppermute | solution.py:67
  43.6 19.0 %collective-permute-start.8 = (bf16[128,2560]{1,0:T(8,128)(2,1)}, bf16[128,2560]{1,0:T(8,128)(2,1)S(1)}, u32[]{:S(2)}, u32[]{:S(2)}) collective-permute-start(bf16[128,2560]{1,0:T(8,128)(2,1)} %collective-permute-done.7), channel_id=1, source_target_pairs={{0,1},{1,0},{2,3},{3,2},{4,5},{5,4},{6,7},{7,6},{8,9},{9,8},{10,11... | collective-permute-start | bytes 1966088 | tf_op jit(solution)/shard_map/ppermute | solution.py:67
  49.5 29.7 %collective-permute-start.16 = (bf16[128,2560]{1,0:T(8,128)(2,1)}, bf16[128,2560]{1,0:T(8,128)(2,1)}, u32[]{:S(2)}, u32[]{:S(2)}) collective-permute-start(bf16[128,2560]{1,0:T(8,128)(2,1)} %collective-permute-done.7), channel_id=1, source_target_pairs={{0,8},{8,16},{16,24},{24,0},{1,9},{9,17},{17,25},{25,1},{2,10},{10... | collective-permute-start | bytes 1966088 | tf_op jit(solution)/shard_map/ppermute | solution.py:67
  62.6 67.1 %collective-permute-start.6 = (f32[2,64,2560]{2,1,0:T(8,128)}, f32[2,64,2560]{2,1,0:T(8,128)}, u32[]{:S(2)}, u32[]{:S(2)}) collective-permute-start(f32[2,64,2560]{2,1,0:T(8,128)} %dynamic-slice_bitcast_fusion.5), channel_id=1, source_target_pairs={{0,2},{2,0},{4,6},{6,4},{1,3},{3,1},{5,7},{7,5},{8,10},{10,8},{12,... | collective-permute-start | bytes 3932168 | tf_op jit(solution)/shard_map/ppermute | solution.py:70
  62.6 7.2 %copy-start.4 = (bf16[256,2560]{1,0:T(8,128)(2,1)}, bf16[256,2560]{1,0:T(8,128)(2,1)S(1)}, u32[]{:S(2)}) copy-start(bf16[256,2560]{1,0:T(8,128)(2,1)S(1)} %constant_dynamic-update-slice_fusion.2.refs_5_) | copy-start | bytes 3932164
  71.8 60.3 %collective-permute-start.9 = (f32[2,64,2560]{2,1,0:T(8,128)}, f32[2,64,2560]{2,1,0:T(8,128)}, u32[]{:S(2)}, u32[]{:S(2)}) collective-permute-start(f32[2,64,2560]{2,1,0:T(8,128)} %dynamic-slice_bitcast_fusion.4), channel_id=1, source_target_pairs={{0,2},{2,0},{4,6},{6,4},{1,3},{3,1},{5,7},{7,5},{8,10},{10,8},{12,... | collective-permute-start | bytes 3932168 | tf_op jit(solution)/shard_map/ppermute | solution.py:70
  76.0 42.8 %collective-permute-start.2 = (bf16[64,5120]{1,0:T(8,128)(2,1)S(1)}, bf16[64,5120]{1,0:T(8,128)(2,1)S(1)}, u32[]{:S(2)}, u32[]{:S(2)}) collective-permute-start(bf16[64,5120]{1,0:T(8,128)(2,1)S(1)} %pad_maximum_fusion.2), channel_id=1, source_target_pairs={{0,4},{2,6},{4,0},{6,2},{1,5},{3,7},{5,1},{7,3},{8,12},{10,14},{12... | collective-permute-start | bytes 1966088 | tf_op jit(solution)/shard_map/ppermute | solution.py:75
  77.6 17.8 %collective-permute-start.14 = (bf16[128,2560]{1,0:T(8,128)(2,1)}, bf16[128,2560]{1,0:T(8,128)(2,1)S(1)}, u32[]{:S(2)}, u32[]{:S(2)}) collective-permute-start(bf16[128,2560]{1,0:T(8,128)(2,1)} %collective-permute-done.13), channel_id=1, source_target_pairs={{0,1},{1,0},{2,3},{3,2},{4,5},{5,4},{6,7},{7,6},{8,9},{9,8},{10,11... | collective-permute-start | bytes 1966088 | tf_op jit(solution)/shard_map/ppermute | solution.py:67
  79.1 29.6 %collective-permute-start.17 = (bf16[128,2560]{1,0:T(8,128)(2,1)}, bf16[128,2560]{1,0:T(8,128)(2,1)S(1)}, u32[]{:S(2)}, u32[]{:S(2)}) collective-permute-start(bf16[128,2560]{1,0:T(8,128)(2,1)} %collective-permute-done.16), channel_id=1, source_target_pairs={{0,1},{1,0},{2,3},{3,2},{4,5},{5,4},{6,7},{7,6},{8,9},{9,8},{10,11... | collective-permute-start | bytes 1966088 | tf_op jit(solution)/shard_map/ppermute | solution.py:67
  95.4 26.3 %collective-permute-start.22 = (bf16[128,2560]{1,0:T(8,128)(2,1)}, bf16[128,2560]{1,0:T(8,128)(2,1)}, u32[]{:S(2)}, u32[]{:S(2)}) collective-permute-start(bf16[128,2560]{1,0:T(8,128)(2,1)} %collective-permute-done.13), channel_id=1, source_target_pairs={{0,8},{8,16},{16,24},{24,0},{1,9},{9,17},{17,25},{25,1},{2,10},{10... | collective-permute-start | bytes 1966088 | tf_op jit(solution)/shard_map/ppermute | solution.py:67
  104.1 13.4 %copy-start.20 = (f32[256,2560]{1,0:T(8,128)}, f32[256,2560]{1,0:T(8,128)S(1)}, u32[]{:S(2)}) copy-start(f32[256,2560]{1,0:T(8,128)S(1)} %fusion.51) | copy-start | bytes 7864324
  108.7 18.3 %collective-permute-start.25 = (bf16[128,2560]{1,0:T(8,128)(2,1)}, bf16[128,2560]{1,0:T(8,128)(2,1)}, u32[]{:S(2)}, u32[]{:S(2)}) collective-permute-start(bf16[128,2560]{1,0:T(8,128)(2,1)} %collective-permute-done.16), channel_id=1, source_target_pairs={{0,8},{8,16},{16,24},{24,0},{1,9},{9,17},{17,25},{25,1},{2,10},{10... | collective-permute-start | bytes 1966088 | tf_op jit(solution)/shard_map/ppermute | solution.py:67
  110.3 7.2 %copy-start.6 = (bf16[256,2560]{1,0:T(8,128)(2,1)}, bf16[256,2560]{1,0:T(8,128)(2,1)S(1)}, u32[]{:S(2)}) copy-start(bf16[256,2560]{1,0:T(8,128)(2,1)S(1)} %constant_dynamic-update-slice_fusion.6.refs_6_) | copy-start | bytes 3932164
  118.8 40.1 %collective-permute-start.15 = (f32[2,64,2560]{2,1,0:T(8,128)}, f32[2,64,2560]{2,1,0:T(8,128)}, u32[]{:S(2)}, u32[]{:S(2)}) collective-permute-start(f32[2,64,2560]{2,1,0:T(8,128)} %dynamic-slice_bitcast_fusion.3), channel_id=1, source_target_pairs={{0,2},{2,0},{4,6},{6,4},{1,3},{3,1},{5,7},{7,5},{8,10},{10,8},{12,... | collective-permute-start | bytes 3932168 | tf_op jit(solution)/shard_map/ppermute | solution.py:70
  120.2 99.0 %all-gather.7.cloned.1.call-start = ((), (), s32[]{:S(2)}) async-start(), calls=%async_computation.1 | async-start | bytes 3276800 | tf_op jit(solution)/shard_map/all_gather | solution.py:125
  120.4 9.9 %copy-start.19 = (f32[256,2560]{1,0:T(8,128)S(1)}, f32[256,2560]{1,0:T(8,128)}, u32[]{:S(2)}) copy-start(f32[256,2560]{1,0:T(8,128)} %copy-done.18) | copy-start | bytes 7864324
  121.7 39.2 %collective-permute-start.18 = (f32[2,64,2560]{2,1,0:T(8,128)}, f32[2,64,2560]{2,1,0:T(8,128)S(1)}, u32[]{:S(2)}, u32[]{:S(2)}) collective-permute-start(f32[2,64,2560]{2,1,0:T(8,128)} %dynamic-slice_bitcast_fusion.2), channel_id=1, source_target_pairs={{0,2},{2,0},{4,6},{6,4},{1,3},{3,1},{5,7},{7,5},{8,10},{10,8},{12,... | collective-permute-start | bytes 3932168 | tf_op jit(solution)/shard_map/ppermute | solution.py:70
  127.0 17.9 %collective-permute-start.23 = (bf16[128,2560]{1,0:T(8,128)(2,1)}, bf16[128,2560]{1,0:T(8,128)(2,1)S(1)}, u32[]{:S(2)}, u32[]{:S(2)}) collective-permute-start(bf16[128,2560]{1,0:T(8,128)(2,1)} %collective-permute-done.22), channel_id=1, source_target_pairs={{0,1},{1,0},{2,3},{3,2},{4,5},{5,4},{6,7},{7,6},{8,9},{9,8},{10,11... | collective-permute-start | bytes 1966088 | tf_op jit(solution)/shard_map/ppermute | solution.py:67
  129.7 26.8 %collective-permute-start.26 = (bf16[128,2560]{1,0:T(8,128)(2,1)}, bf16[128,2560]{1,0:T(8,128)(2,1)S(1)}, u32[]{:S(2)}, u32[]{:S(2)}) collective-permute-start(bf16[128,2560]{1,0:T(8,128)(2,1)} %collective-permute-done.25), channel_id=1, source_target_pairs={{0,1},{1,0},{2,3},{3,2},{4,5},{5,4},{6,7},{7,6},{8,9},{9,8},{10,11... | collective-permute-start | bytes 1966088 | tf_op jit(solution)/shard_map/ppermute | solution.py:67
  134.1 23.4 %collective-permute-start.10 = (bf16[64,5120]{1,0:T(8,128)(2,1)S(1)}, bf16[64,5120]{1,0:T(8,128)(2,1)S(1)}, u32[]{:S(2)}, u32[]{:S(2)}) collective-permute-start(bf16[64,5120]{1,0:T(8,128)(2,1)S(1)} %pad_maximum_fusion.4), channel_id=1, source_target_pairs={{0,4},{2,6},{4,0},{6,2},{1,5},{3,7},{5,1},{7,3},{8,12},{10,14},{12... | collective-permute-start | bytes 1966088 | tf_op jit(solution)/shard_map/ppermute | solution.py:75
  154.0 35.4 %collective-permute-start.24 = (f32[2,64,2560]{2,1,0:T(8,128)}, f32[2,64,2560]{2,1,0:T(8,128)}, u32[]{:S(2)}, u32[]{:S(2)}) collective-permute-start(f32[2,64,2560]{2,1,0:T(8,128)} %dynamic-slice_bitcast_fusion.1), channel_id=1, source_target_pairs={{0,2},{2,0},{4,6},{6,4},{1,3},{3,1},{5,7},{7,5},{8,10},{10,8},{12,... | collective-permute-start | bytes 3932168 | tf_op jit(solution)/shard_map/ppermute | solution.py:70
  158.9 70.3 %all-gather.9.cloned.1.call-start = ((), (), s32[]{:S(2)}) async-start(), calls=%async_computation.2 | async-start | bytes 3276800 | tf_op jit(solution)/shard_map/all_gather | solution.py:125
  161.7 26.2 %collective-permute-start.19 = (bf16[64,5120]{1,0:T(8,128)(2,1)S(1)}, bf16[64,5120]{1,0:T(8,128)(2,1)S(1)}, u32[]{:S(2)}, u32[]{:S(2)}) collective-permute-start(bf16[64,5120]{1,0:T(8,128)(2,1)S(1)} %pad_maximum_fusion.6), channel_id=1, source_target_pairs={{0,4},{2,6},{4,0},{6,2},{1,5},{3,7},{5,1},{7,3},{8,12},{10,14},{12... | collective-permute-start | bytes 1966088 | tf_op jit(solution)/shard_map/ppermute | solution.py:75
  171.2 20.5 %collective-permute-start.27 = (f32[2,64,2560]{2,1,0:T(8,128)}, f32[2,64,2560]{2,1,0:T(8,128)}, u32[]{:S(2)}, u32[]{:S(2)}) collective-permute-start(f32[2,64,2560]{2,1,0:T(8,128)} %dynamic-slice_bitcast_fusion), channel_id=1, source_target_pairs={{0,2},{2,0},{4,6},{6,4},{1,3},{3,1},{5,7},{7,5},{8,10},{10,8},{12,... | collective-permute-start | bytes 3932168 | tf_op jit(solution)/shard_map/ppermute | solution.py:70
  189.3 70.7 %all-gather.11.cloned.1.call-start = ((), (), s32[]{:S(2)}) async-start(), calls=%async_computation.3 | async-start | bytes 3276800 | tf_op jit(solution)/shard_map/all_gather | solution.py:125
  193.8 12.9 %collective-permute-start.28 = (bf16[64,5120]{1,0:T(8,128)(2,1)S(1)}, bf16[64,5120]{1,0:T(8,128)(2,1)S(1)}, u32[]{:S(2)}, u32[]{:S(2)}) collective-permute-start(bf16[64,5120]{1,0:T(8,128)(2,1)S(1)} %pad_maximum_fusion.8), channel_id=1, source_target_pairs={{0,4},{2,6},{4,0},{6,2},{1,5},{3,7},{5,1},{7,3},{8,12},{10,14},{12... | collective-permute-start | bytes 1966088 | tf_op jit(solution)/shard_map/ppermute | solution.py:75
  217.7 97.2 %collective-permute-start.3 = (bf16[128,2560]{1,0:T(8,128)(2,1)}, bf16[128,2560]{1,0:T(8,128)(2,1)S(1)}, u32[]{:S(2)}, u32[]{:S(2)}) collective-permute-start(bf16[128,2560]{1,0:T(8,128)(2,1)} %slice.169), channel_id=1, source_target_pairs={{0,1},{1,0},{2,3},{3,2},{4,5},{5,4},{6,7},{7,6},{8,9},{9,8},{10,11... | collective-permute-start | bytes 1966088 | tf_op jit(solution)/shard_map/ppermute | solution.py:67
  228.7 18.0 %collective-permute-start.11 = (bf16[128,2560]{1,0:T(8,128)(2,1)}, bf16[128,2560]{1,0:T(8,128)(2,1)}, u32[]{:S(2)}, u32[]{:S(2)}) collective-permute-start(bf16[128,2560]{1,0:T(8,128)(2,1)} %slice.168), channel_id=1, source_target_pairs={{0,1},{1,0},{2,3},{3,2},{4,5},{5,4},{6,7},{7,6},{8,9},{9,8},{10,11... | collective-permute-start | bytes 1966088 | tf_op jit(solution)/shard_map/ppermute | solution.py:67
  229.2 17.5 %copy-start.36 = (f32[256,2560]{1,0:T(8,128)S(1)}, f32[256,2560]{1,0:T(8,128)}, u32[]{:S(2)}) copy-start(f32[256,2560]{1,0:T(8,128)} %copy-done.35) | copy-start | bytes 7864324
  237.1 19.5 %collective-permute-start.20 = (bf16[128,2560]{1,0:T(8,128)(2,1)S(1)}, bf16[128,2560]{1,0:T(8,128)(2,1)S(1)}, u32[]{:S(2)}, u32[]{:S(2)}) collective-permute-start(bf16[128,2560]{1,0:T(8,128)(2,1)S(1)} %slice.167), channel_id=1, source_target_pairs={{0,1},{1,0},{2,3},{3,2},{4,5},{5,4},{6,7},{7,6},{8,9},{9,8},{10,11... | collective-permute-start | bytes 1966088 | tf_op jit(solution)/shard_map/ppermute | solution.py:67
  248.7 66.2 %collective-permute-start.12 = (bf16[128,2560]{1,0:T(8,128)(2,1)}, bf16[128,2560]{1,0:T(8,128)(2,1)}, u32[]{:S(2)}, u32[]{:S(2)}) collective-permute-start(bf16[128,2560]{1,0:T(8,128)(2,1)} %fusion.6), channel_id=1, source_target_pairs={{0,24},{8,0},{16,8},{24,16},{1,25},{9,1},{17,9},{25,17},{2,26},{10... | collective-permute-start | bytes 1966088 | tf_op jit(solution)/shard_map/ppermute | solution.py:67
  257.6 57.3 %collective-permute-start.21 = (bf16[128,2560]{1,0:T(8,128)(2,1)}, bf16[128,2560]{1,0:T(8,128)(2,1)}, u32[]{:S(2)}, u32[]{:S(2)}) collective-permute-start(bf16[128,2560]{1,0:T(8,128)(2,1)} %fusion.3), channel_id=1, source_target_pairs={{0,16},{8,24},{16,0},{24,8},{1,17},{9,25},{17,1},{25,9},{2,18},{10... | collective-permute-start | bytes 1966088 | tf_op jit(solution)/shard_map/ppermute | solution.py:67
  260.1 10.2 %copy-start.1 = (bf16[256,2560]{1,0:T(8,128)(2,1)S(1)}, bf16[256,2560]{1,0:T(8,128)(2,1)}, u32[]{:S(2)}) copy-start(bf16[256,2560]{1,0:T(8,128)(2,1)} %copy-done) | copy-start | bytes 3932164
  260.1 10.2 %copy-start.5 = (bf16[256,2560]{1,0:T(8,128)(2,1)S(1)}, bf16[256,2560]{1,0:T(8,128)(2,1)}, u32[]{:S(2)}) copy-start(bf16[256,2560]{1,0:T(8,128)(2,1)} %copy-done.4) | copy-start | bytes 3932164
  260.1 10.2 %copy-start.7 = (bf16[256,2560]{1,0:T(8,128)(2,1)S(1)}, bf16[256,2560]{1,0:T(8,128)(2,1)}, u32[]{:S(2)}) copy-start(bf16[256,2560]{1,0:T(8,128)(2,1)} %copy-done.6) | copy-start | bytes 3932164
  268.8 26.4 %collective-permute-start.29 = (bf16[128,2560]{1,0:T(8,128)(2,1)S(1)}, bf16[128,2560]{1,0:T(8,128)(2,1)S(1)}, u32[]{:S(2)}, u32[]{:S(2)}) collective-permute-start(bf16[128,2560]{1,0:T(8,128)(2,1)S(1)} %slice.166), channel_id=1, source_target_pairs={{0,1},{1,0},{2,3},{3,2},{4,5},{5,4},{6,7},{7,6},{8,9},{9,8},{10,11... | collective-permute-start | bytes 1966088 | tf_op jit(solution)/shard_map/ppermute | solution.py:67
  277.2 17.9 %copy-start.38 = (f32[256,2560]{1,0:T(8,128)S(1)}, f32[256,2560]{1,0:T(8,128)}, u32[]{:S(2)}) copy-start(f32[256,2560]{1,0:T(8,128)} %copy-done.37) | copy-start | bytes 7864324
  277.2 19.6 %copy-start.11 = (bf16[256,2560]{1,0:T(8,128)(2,1)S(1)}, bf16[256,2560]{1,0:T(8,128)(2,1)}, u32[]{:S(2)}) copy-start(bf16[256,2560]{1,0:T(8,128)(2,1)} %copy-done.10) | copy-start | bytes 3932164
  277.2 19.6 %copy-start.13 = (bf16[256,5120]{1,0:T(8,128)(2,1)S(1)}, bf16[256,5120]{1,0:T(8,128)(2,1)}, u32[]{:S(2)}) copy-start(bf16[256,5120]{1,0:T(8,128)(2,1)} %all-gather.5.cloned.1.call-done.refs_4_.refs_0_) | copy-start | bytes 7864324
  277.3 19.6 %copy-start.15 = (bf16[256,5120]{1,0:T(8,128)(2,1)S(1)}, bf16[256,5120]{1,0:T(8,128)(2,1)}, u32[]{:S(2)}) copy-start(bf16[256,5120]{1,0:T(8,128)(2,1)} %all-gather.7.cloned.1.call-done.refs_5_.refs_1_) | copy-start | bytes 7864324
  295.3 19.6 %copy-start.40 = (f32[256,2560]{1,0:T(8,128)S(1)}, f32[256,2560]{1,0:T(8,128)}, u32[]{:S(2)}) copy-start(f32[256,2560]{1,0:T(8,128)} %copy-done.39) | copy-start | bytes 7864324
  295.3 19.6 %collective-permute-start.30 = (bf16[128,2560]{1,0:T(8,128)(2,1)S(1)}, bf16[128,2560]{1,0:T(8,128)(2,1)S(1)}, u32[]{:S(2)}, u32[]{:S(2)}) collective-permute-start(bf16[128,2560]{1,0:T(8,128)(2,1)S(1)} %fusion), channel_id=1, source_target_pairs={{0,8},{8,16},{16,24},{24,0},{1,9},{9,17},{17,25},{25,1},{2,10},{10... | collective-permute-start | bytes 1966088 | tf_op jit(solution)/shard_map/ppermute | solution.py:67
  (29 other events, 82.1 us)
Sparse Core Ops, SparseCore 0:
  120.3 32.6 all-gather.4
  159.0 34.4 all-gather.6
  195.1 26.1 all-gather.8
  223.2 25.5 all-gather.10

commit v2 on v1

--- a/solution.py
+++ b/solution.py
@@ -115,6 +115,23 @@
             held = [held[0] + got[:, :hidden], held[1] + got[:, hidden:]]
         return held
 
+    def in_order(blocks, at):
+        n = len(blocks)
+        ordered = []
+        for j in range(n):
+            k, block = (j - at) % n, blocks[0]
+            for other in range(1, n):
+                block = jnp.where(k == other, blocks[other], block)
+            ordered.append(block)
+        return ordered
+
+    def con_gather(share):
+        blocks = [share] + [shift_outer(share, -k) for k in range(1, outer)]
+        held = jnp.concatenate(in_order(blocks, co), axis=0)
+        halves = [held] + [shift_inner(held, -k) for k in range(1, inner)]
+        halves = [a.reshape(outer, 1, shard // C, -1) for a in in_order(halves, ci)]
+        return jnp.concatenate(halves, axis=1).reshape(shard, -1)
+
     both, result = [], None
     for k in range(T):
         pre = jnp.dot(toks[k], weight_in, preferred_element_type=f32)
@@ -122,7 +139,7 @@
             grads[k], weight_out, (((1,), (1,)), ((), ())), preferred_element_type=f32
         )
         share = jnp.concatenate(gelu_parts(*con_sum(pre, grad)), axis=1)
-        chunk = lax.all_gather(share, "con", axis=0, tiled=True)
+        chunk = con_gather(share)
         both.append(chunk)
         back = lax.dot_general(
             chunk[:, hidden:], weight_in, (((1,), (1,)), ((), ())), preferred_element_type=f32

time: 325 us -> 375 us (1.15)
  waiting for transfers between devices: 88.3 us -> 136 us
  other arithmetic: 24 us -> 37.4 us
  between operations: 14.6 us -> 1.38 us
  matrix products: 85.3 us -> 90.7 us
    ppermute x4 -> x8, waiting for transfers between devices: 28.4 us -> 61.3 us  [shift_outer(): lax.ppermute(a, 'con', [(i, (i // inner + by) % outer * inner + i % inner...]
    ppermute x19, waiting for transfers between devices: 59.8 us -> 74.2 us  [shift(): return lax.ppermute(a, axis, [(i, (i + by) % size) for i in range(size)])]
    unnamed x90 -> x54, local copies, waits for them, and re-layouts: 24.7 us -> 15.8 us
    ppermute x19, starting transfers between devices: 31.1 us -> 22.8 us  [shift(): return lax.ppermute(a, axis, [(i, (i + by) % size) for i in range(size)])]
    select_n x0 -> x6, other arithmetic: none -> 8.23 us  [in_order(): block = jnp.where(k == other, blocks[other], block)]
    ppermute x4 -> x8, starting transfers between devices: 3.01 us -> 10.4 us  [shift_outer(): lax.ppermute(a, 'con', [(i, (i // inner + by) % outer * inner + i % inner...]
    slice x4, local copies, waits for them, and re-layouts: 1.95 us -> 8.04 us  [per_device(): sent = back[j * rows:(j + 1) * rows].astype(bf16)]
  transfers between devices with their start and end apart: 35 -> 39, of which waited for: 13 -> 14; matrix products, arithmetic and copies ran while one was open for 39% -> 41% of each run, Pallas kernels for 11% -> 10%
where the time goes in v2:
time: 375 us; the launch traced here: 373 us
  waiting for transfers between devices  136 us (36%)
  matrix products  90.7 us (24%)
  local copies, waits for them, and re-layouts  37.5 us (10%)
  other arithmetic  37.4 us (10%)
  Pallas kernels  35.9 us (10%)
  starting transfers between devices  35 us (9%)
    ppermute x19, waiting for transfers between devices, shift(): return lax.ppermute(a, axis, [(i, (i + by) % size) for i in range(size)])  74.2 us
    ppermute x8, waiting for transfers between devices, shift_outer(): lax.ppermute(a, 'con', [(i, (i // inner + by) % outer * inner + i % inner...  61.3 us
    pallas_call x2, Pallas kernels, summed_outer(): pl.pallas_call(functools.partial(grad_kernel, chunks, width), grid=(left_...  35.9 us
    dot_general x4, matrix products, per_device(): lax.dot_general(chunk[:, hidden:], weight_in, (((1,), (1,)), ((), ())), p...  32.9 us
    dot_general x4, matrix products, per_device(): lax.dot_general(grads[k], weight_out, (((1,), (1,)), ((), ())), preferred...  29.8 us
    dot_general x4, matrix products, per_device(): pre = jnp.dot(toks[k], weight_in, preferred_element_type=f32)  28.1 us
    ppermute x19, starting transfers between devices, shift(): return lax.ppermute(a, axis, [(i, (i + by) % size) for i in range(size)])  22.8 us
    unnamed x54, local copies, waits for them, and re-layouts  15.8 us
  transfers between devices with their start and end apart: 39, of which 14 were waited for; matrix products, arithmetic and copies ran while one was open for 41% of the time, Pallas kernels for 10%

profile of v2, /device:TPU:0, one launch (start us, length us, event | category | flops | bytes accessed | tf_op | source)
XLA Modules:
  0.0 373.4 jit_solution(3419474834708252465)
XLA Ops:
  0.7 2.2 constant_dynamic-slice_fusion.3
  2.9 3.0 collective-permute-start.6
  5.9 6.8 %fusion.48 = f32[256,2560]{1,0:T(8,128)S(1)} fusion(bf16[2560,2560]{1,0:T(8,128)(2,1)} %param.6, bf16[128,2560]{1,0:T(8,128)(2,1)S(1)} %get-tuple-element.28, bf16[128,2560]{1,0:T(8,128)(2,1)} %get-tuple-element.27), kind=kOutput, calls=%fused_computation.150 | convolution fusion | flops 3358064640 | bytes 17039360 | tf_op jit(solution)/shard_map/dot_general | solution.py:137
  15.5 1.6 collective-permute-start.9
  17.0 6.8 %fusion.47 = f32[256,2560]{1,0:T(8,128)S(1)} fusion(bf16[2560,2560]{1,0:T(8,128)(2,1)} %param.7, bf16[128,2560]{1,0:T(8,128)(2,1)S(1)} %get-tuple-element.30, bf16[128,2560]{1,0:T(8,128)(2,1)} %get-tuple-element.29), kind=kOutput, calls=%fused_computation.149 | convolution fusion | flops 3358064640 | bytes 17039360 | tf_op jit(solution)/shard_map/dot_general | solution.py:138
  25.8 2.5 pad_maximum_fusion.5.refs_4_
  28.4 2.2 pad_maximum_fusion.4.refs_0_
  32.1 1.6 collective-permute-start.17
  33.7 3.4 collective-permute-done.9
  37.0 2.5 collective-permute-start.10
  41.9 1.6 bitcast_add_fusion.7
  48.4 7.1 %fusion.49 = f32[256,2560]{1,0:T(8,128)S(1)} fusion(bf16[256,2560]{1,0:T(8,128)(2,1)S(1)} %constant_dynamic-update-slice_fusion.refs_1_, bf16[2560,2560]{1,0:T(8,128)(2,1)} %param.6), kind=kOutput, calls=%fused_computation.151 | convolution fusion | flops 3355443200 | bytes 17039360 | tf_op jit(solution)/shard_map/dot_general | solution.py:137
  56.7 5.3 %collective-permute-done.10 = bf16[128,2560]{1,0:T(8,128)(2,1)S(1)} collective-permute-done((bf16[128,2560]{1,0:T(8,128)(2,1)}, bf16[128,2560]{1,0:T(8,128)(2,1)S(1)}, u32[]{:S(2)}, u32[]{:S(2)}) %collective-permute-start.10) | collective-permute-done | bytes 655392 | tf_op jit(solution)/shard_map/ppermute | solution.py:67
  62.0 7.1 %fusion.50 = f32[256,2560]{1,0:T(8,128)S(1)} fusion(bf16[256,2560]{1,0:T(8,128)(2,1)S(1)} %constant_dynamic-update-slice_fusion.2.refs_5_, bf16[2560,2560]{1,0:T(8,128)(2,1)} %param.7), kind=kOutput, calls=%fused_computation.152 | convolution fusion | flops 3355443200 | bytes 17039360 | tf_op jit(solution)/shard_map/dot_general | solution.py:138
  74.7 13.4 %collective-permute-done.18 = bf16[128,2560]{1,0:T(8,128)(2,1)S(1)} collective-permute-done((bf16[128,2560]{1,0:T(8,128)(2,1)}, bf16[128,2560]{1,0:T(8,128)(2,1)S(1)}, u32[]{:S(2)}, u32[]{:S(2)}) %collective-permute-start.18) | collective-permute-done | bytes 655392 | tf_op jit(solution)/shard_map/ppermute | solution.py:67
  88.1 1.6 collective-permute-start.28
  89.7 7.1 %fusion.51 = f32[256,2560]{1,0:T(8,128)S(1)} fusion(bf16[256,2560]{1,0:T(8,128)(2,1)S(1)} %constant_dynamic-update-slice_fusion.4.refs_2_, bf16[2560,2560]{1,0:T(8,128)(2,1)} %param.6), kind=kOutput, calls=%fused_computation.153 | convolution fusion | flops 3355443200 | bytes 17039360 | tf_op jit(solution)/shard_map/dot_general | solution.py:137
  99.8 2.0 collective-permute-done.21
  103.3 7.1 %fusion.52 = f32[256,2560]{1,0:T(8,128)S(1)} fusion(bf16[256,2560]{1,0:T(8,128)(2,1)S(1)} %constant_dynamic-update-slice_fusion.6.refs_6_, bf16[2560,2560]{1,0:T(8,128)(2,1)} %param.7), kind=kOutput, calls=%fused_computation.154 | convolution fusion | flops 3355443200 | bytes 17039360 | tf_op jit(solution)/shard_map/dot_general | solution.py:138
  114.2 6.1 %collective-permute-done.31 = bf16[128,2560]{1,0:T(8,128)(2,1)} collective-permute-done((bf16[128,2560]{1,0:T(8,128)(2,1)}, bf16[128,2560]{1,0:T(8,128)(2,1)}, u32[]{:S(2)}, u32[]{:S(2)}) %collective-permute-start.31) | collective-permute-done | bytes 655392 | tf_op jit(solution)/shard_map/ppermute | solution.py:67
  121.4 1.6 collective-permute-start.29
  126.8 12.4 %collective-permute-done.29 = bf16[128,2560]{1,0:T(8,128)(2,1)S(1)} collective-permute-done((bf16[128,2560]{1,0:T(8,128)(2,1)}, bf16[128,2560]{1,0:T(8,128)(2,1)S(1)}, u32[]{:S(2)}, u32[]{:S(2)}) %collective-permute-start.29) | collective-permute-done | bytes 655392 | tf_op jit(solution)/shard_map/ppermute | solution.py:67
  140.7 7.1 %fusion.53 = f32[256,2560]{1,0:T(8,128)S(1)} fusion(bf16[256,2560]{1,0:T(8,128)(2,1)S(1)} %constant_dynamic-update-slice_fusion.8.refs_3_, bf16[2560,2560]{1,0:T(8,128)(2,1)} %param.6), kind=kOutput, calls=%fused_computation.155 | convolution fusion | flops 3355443200 | bytes 17039360 | tf_op jit(solution)/shard_map/dot_general | solution.py:137
  149.0 3.8 %collective-permute-done.32 = bf16[128,2560]{1,0:T(8,128)(2,1)S(1)} collective-permute-done((bf16[128,2560]{1,0:T(8,128)(2,1)}, bf16[128,2560]{1,0:T(8,128)(2,1)S(1)}, u32[]{:S(2)}, u32[]{:S(2)}) %collective-permute-start.32) | collective-permute-done | bytes 655392 | tf_op jit(solution)/shard_map/ppermute | solution.py:67
  152.9 8.6 %fusion.54 = f32[256,2560]{1,0:T(8,128)} fusion(bf16[256,2560]{1,0:T(8,128)(2,1)S(1)} %constant_dynamic-update-slice_fusion.10.refs_7_, bf16[2560,2560]{1,0:T(8,128)(2,1)} %param.7), kind=kOutput, calls=%fused_computation.156 | convolution fusion | flops 3355443200 | bytes 17039360 | tf_op jit(solution)/shard_map/dot_general | solution.py:138
  163.6 1.6 bitcast_add_fusion.3
  171.1 13.9 %collective-permute-done.23 = bf16[64,5120]{1,0:T(8,128)(2,1)S(1)} collective-permute-done((bf16[64,5120]{1,0:T(8,128)(2,1)S(1)}, bf16[64,5120]{1,0:T(8,128)(2,1)S(1)}, u32[]{:S(2)}, u32[]{:S(2)}) %collective-permute-start.23) | collective-permute-done | bytes 655392 | tf_op jit(solution)/shard_map/ppermute | solution.py:75
  189.7 9.4 %collective-permute-done.13 = bf16[64,5120]{1,0:T(8,128)(2,1)S(1)} collective-permute-done((bf16[64,5120]{1,0:T(8,128)(2,1)S(1)}, bf16[64,5120]{1,0:T(8,128)(2,1)S(1)}, u32[]{:S(2)}, u32[]{:S(2)}) %collective-permute-start.13) | collective-permute-done | bytes 655392 | tf_op jit(solution)/shard_map/ppermute | solution.py:75
  199.0 1.6 broadcast_select_fusion.14
  200.7 25.5 %collective-permute-done.34 = bf16[64,5120]{1,0:T(8,128)(2,1)S(1)} collective-permute-done((bf16[64,5120]{1,0:T(8,128)(2,1)S(1)}, bf16[64,5120]{1,0:T(8,128)(2,1)S(1)}, u32[]{:S(2)}, u32[]{:S(2)}) %collective-permute-start.34) | collective-permute-done | bytes 655392 | tf_op jit(solution)/shard_map/ppermute | solution.py:75
  230.1 12.5 %collective-permute-done.35 = bf16[64,5120]{1,0:T(8,128)(2,1)S(1)} collective-permute-done((bf16[64,5120]{1,0:T(8,128)(2,1)S(1)}, bf16[64,5120]{1,0:T(8,128)(2,1)S(1)}, u32[]{:S(2)}, u32[]{:S(2)}) %collective-permute-start.35) | collective-permute-done | bytes 655392 | tf_op jit(solution)/shard_map/ppermute | solution.py:75
  245.6 8.4 %fusion.7 = f32[256,2560]{1,0:T(8,128)} fusion(bf16[2560,2560]{1,0:T(8,128)(2,1)} %param.6, bf16[256,5120]{1,0:T(8,128)(2,1)S(1)} %bitcast.118), kind=kOutput, calls=%fused_computation.17 | convolution fusion | flops 3355443200 | bytes 17039360 | tf_op jit(solution)/shard_map/dot_general | solution.py:144
  254.0 2.2 slice.168
  257.8 1.8 broadcast_select_fusion.7
  259.8 8.2 %fusion.13 = f32[256,2560]{1,0:T(8,128)} fusion(bf16[2560,2560]{1,0:T(8,128)(2,1)} %param.6, bf16[256,5120]{1,0:T(8,128)(2,1)S(1)} %bitcast.121), kind=kOutput, calls=%fused_computation.25 | convolution fusion | flops 3355443200 | bytes 17039360 | tf_op jit(solution)/shard_map/dot_general | solution.py:144
  268.0 2.2 slice.169
  270.7 2.9 collective-permute-done.15
  273.5 2.5 fusion.6
  276.4 1.9 broadcast_select_fusion.5
  278.6 8.2 %fusion.4 = f32[256,2560]{1,0:T(8,128)} fusion(bf16[2560,2560]{1,0:T(8,128)(2,1)} %param.6, bf16[256,5120]{1,0:T(8,128)(2,1)S(1)} %bitcast.124), kind=kOutput, calls=%fused_computation.12 | convolution fusion | flops 3355443200 | bytes 17039360 | tf_op jit(solution)/shard_map/dot_general | solution.py:144
  286.8 2.2 slice.167
  289.0 2.2 collective-permute-start.26
  291.2 1.9 broadcast_select_fusion.4
  293.3 8.2 %fusion.1 = f32[256,2560]{1,0:T(8,128)} fusion(bf16[2560,2560]{1,0:T(8,128)(2,1)} %param.6, bf16[256,5120]{1,0:T(8,128)(2,1)S(1)} %bitcast.127), kind=kOutput, calls=%fused_computation.7 | convolution fusion | flops 3355443200 | bytes 17039360 | tf_op jit(solution)/shard_map/dot_general | solution.py:144
  308.2 17.9 %shard_map.68 = f32[2560,2560]{1,0:T(8,128)} custom-call(bf16[256,5120]{1,0:T(8,128)(2,1)S(1)} %bitcast.122, bf16[256,5120]{1,0:T(8,128)(2,1)S(1)} %bitcast.119, bf16[256,5120]{1,0:T(8,128)(2,1)S(1)} %bitcast.125, bf16[256,5120]{1,0:T(8,128)(2,1)S(1)} %bitcast.128, bf16[256,2560]{1,0:T(8,128)(2,1)S(1)} %copy-done.1, bf16[256,2560]{1,0:T(8,128)(2,1)S(1)} %copy-done.7, ...), custom_call_target="tpu_custom_call" | custom-call | flops 13421772800 | bytes 36700160 | tf_op jit(solution)/shard_map/pallas_call | solution.py:40
  329.4 18.0 %shard_map.67 = f32[2560,2560]{1,0:T(8,128)} custom-call(bf16[256,2560]{1,0:T(8,128)(2,1)S(1)} %copy-done, bf16[256,2560]{1,0:T(8,128)(2,1)S(1)} %copy-done.11, bf16[256,2560]{1,0:T(8,128)(2,1)S(1)} %copy-done.13, bf16[256,2560]{1,0:T(8,128)(2,1)S(1)} %copy-done.5, bf16[256,5120]{1,0:T(8,128)(2,1)S(1)} %bitcast.123, bf16[256,5120]{1,0:T(8,128)(2,1)S(1)} %bitcast.120, ...), custom_call_target="tpu_custom_call" | custom-call | flops 13421772800 | bytes 36700160 | tf_op jit(solution)/shard_map/pallas_call | solution.py:40
  347.4 23.7 %collective-permute-done.27 = bf16[128,2560]{1,0:T(8,128)(2,1)S(1)} collective-permute-done((bf16[128,2560]{1,0:T(8,128)(2,1)S(1)}, bf16[128,2560]{1,0:T(8,128)(2,1)S(1)}, u32[]{:S(2)}, u32[]{:S(2)}) %collective-permute-start.27) | collective-permute-done | bytes 655392 | tf_op jit(solution)/shard_map/ppermute | solution.py:67
  371.1 2.3 fusion.12
  (170 shorter events, 68.3 us)
Async XLA Ops:
  2.9 27.7 %collective-permute-start.6 = (bf16[128,2560]{1,0:T(8,128)(2,1)}, bf16[128,2560]{1,0:T(8,128)(2,1)}, u32[]{:S(2)}, u32[]{:S(2)}) collective-permute-start(bf16[128,2560]{1,0:T(8,128)(2,1)} %get-tuple-element.27), channel_id=1, source_target_pairs={{0,8},{8,16},{16,24},{24,0},{1,9},{9,17},{17,25},{25,1},{2,10},{10... | collective-permute-start | bytes 1966088 | tf_op jit(solution)/shard_map/ppermute | solution.py:67
  13.9 27.8 %collective-permute-start = (f32[2,64,2560]{2,1,0:T(8,128)}, f32[2,64,2560]{2,1,0:T(8,128)}, u32[]{:S(2)}, u32[]{:S(2)}) collective-permute-start(f32[2,64,2560]{2,1,0:T(8,128)} %dynamic-slice_bitcast_fusion.7), channel_id=1, source_target_pairs={{0,2},{2,0},{4,6},{6,4},{1,3},{3,1},{5,7},{7,5},{8,10},{10,8},{12,... | collective-permute-start | bytes 3932168 | tf_op jit(solution)/shard_map/ppermute | solution.py:70
  15.5 8.4 %copy-start.19 = (bf16[128,2560]{1,0:T(8,128)(2,1)}, bf16[128,2560]{1,0:T(8,128)(2,1)S(1)}, u32[]{:S(2)}) copy-start(bf16[128,2560]{1,0:T(8,128)(2,1)S(1)} %get-tuple-element.30) | copy-start | bytes 1966084
  15.5 21.6 %collective-permute-start.9 = (bf16[128,2560]{1,0:T(8,128)(2,1)}, bf16[128,2560]{1,0:T(8,128)(2,1)}, u32[]{:S(2)}, u32[]{:S(2)}) collective-permute-start(bf16[128,2560]{1,0:T(8,128)(2,1)} %get-tuple-element.29), channel_id=1, source_target_pairs={{0,8},{8,16},{16,24},{24,0},{1,9},{9,17},{17,25},{25,1},{2,10},{10... | collective-permute-start | bytes 1966088 | tf_op jit(solution)/shard_map/ppermute | solution.py:67
  25.8 17.7 %collective-permute-start.1 = (f32[2,64,2560]{2,1,0:T(8,128)}, f32[2,64,2560]{2,1,0:T(8,128)}, u32[]{:S(2)}, u32[]{:S(2)}) collective-permute-start(f32[2,64,2560]{2,1,0:T(8,128)} %dynamic-slice_bitcast_fusion.6), channel_id=1, source_target_pairs={{0,2},{2,0},{4,6},{6,4},{1,3},{3,1},{5,7},{7,5},{8,10},{10,8},{12,... | collective-permute-start | bytes 3932168 | tf_op jit(solution)/shard_map/ppermute | solution.py:70
  30.6 17.7 %collective-permute-start.7 = (bf16[128,2560]{1,0:T(8,128)(2,1)}, bf16[128,2560]{1,0:T(8,128)(2,1)S(1)}, u32[]{:S(2)}, u32[]{:S(2)}) collective-permute-start(bf16[128,2560]{1,0:T(8,128)(2,1)} %collective-permute-done.6), channel_id=1, source_target_pairs={{0,1},{1,0},{2,3},{3,2},{4,5},{5,4},{6,7},{7,6},{8,9},{9,8},{10,11... | collective-permute-start | bytes 1966088 | tf_op jit(solution)/shard_map/ppermute | solution.py:67
  32.1 38.3 %collective-permute-start.17 = (bf16[128,2560]{1,0:T(8,128)(2,1)}, bf16[128,2560]{1,0:T(8,128)(2,1)}, u32[]{:S(2)}, u32[]{:S(2)}) collective-permute-start(bf16[128,2560]{1,0:T(8,128)(2,1)} %collective-permute-done.6), channel_id=1, source_target_pairs={{0,8},{8,16},{16,24},{24,0},{1,9},{9,17},{17,25},{25,1},{2,10},{10... | collective-permute-start | bytes 1966088 | tf_op jit(solution)/shard_map/ppermute | solution.py:67
  37.0 24.9 %collective-permute-start.10 = (bf16[128,2560]{1,0:T(8,128)(2,1)}, bf16[128,2560]{1,0:T(8,128)(2,1)S(1)}, u32[]{:S(2)}, u32[]{:S(2)}) collective-permute-start(bf16[128,2560]{1,0:T(8,128)(2,1)} %collective-permute-done.9), channel_id=1, source_target_pairs={{0,1},{1,0},{2,3},{3,2},{4,5},{5,4},{6,7},{7,6},{8,9},{9,8},{10,11... | collective-permute-start | bytes 1966088 | tf_op jit(solution)/shard_map/ppermute | solution.py:67
  41.8 30.1 %collective-permute-start.20 = (bf16[128,2560]{1,0:T(8,128)(2,1)}, bf16[128,2560]{1,0:T(8,128)(2,1)}, u32[]{:S(2)}, u32[]{:S(2)}) collective-permute-start(bf16[128,2560]{1,0:T(8,128)(2,1)} %collective-permute-done.9), channel_id=1, source_target_pairs={{0,8},{8,16},{16,24},{24,0},{1,9},{9,17},{17,25},{25,1},{2,10},{10... | collective-permute-start | bytes 1966088 | tf_op jit(solution)/shard_map/ppermute | solution.py:67
  45.6 51.3 %collective-permute-start.2 = (bf16[64,5120]{1,0:T(8,128)(2,1)S(1)}, bf16[64,5120]{1,0:T(8,128)(2,1)}, u32[]{:S(2)}, u32[]{:S(2)}) collective-permute-start(bf16[64,5120]{1,0:T(8,128)(2,1)S(1)} %pad_maximum_fusion.10), channel_id=1, source_target_pairs={{0,4},{2,6},{4,0},{6,2},{1,5},{3,7},{5,1},{7,3},{8,12},{10,14},{12... | collective-permute-start | bytes 1966088 | tf_op jit(solution)/shard_map/ppermute | solution.py:75
  48.4 7.1 %copy-start.10 = (bf16[256,2560]{1,0:T(8,128)(2,1)}, bf16[256,2560]{1,0:T(8,128)(2,1)S(1)}, u32[]{:S(2)}) copy-start(bf16[256,2560]{1,0:T(8,128)(2,1)S(1)} %constant_dynamic-update-slice_fusion.refs_1_) | copy-start | bytes 3932164
  56.7 64.7 %collective-permute-start.8 = (f32[2,64,2560]{2,1,0:T(8,128)}, f32[2,64,2560]{2,1,0:T(8,128)}, u32[]{:S(2)}, u32[]{:S(2)}) collective-permute-start(f32[2,64,2560]{2,1,0:T(8,128)} %dynamic-slice_bitcast_fusion.5), channel_id=1, source_target_pairs={{0,2},{2,0},{4,6},{6,4},{1,3},{3,1},{5,7},{7,5},{8,10},{10,8},{12,... | collective-permute-start | bytes 3932168 | tf_op jit(solution)/shard_map/ppermute | solution.py:70
  62.0 7.2 %copy-start.6 = (bf16[256,2560]{1,0:T(8,128)(2,1)}, bf16[256,2560]{1,0:T(8,128)(2,1)S(1)}, u32[]{:S(2)}) copy-start(bf16[256,2560]{1,0:T(8,128)(2,1)S(1)} %constant_dynamic-update-slice_fusion.2.refs_5_) | copy-start | bytes 3932164
  70.4 54.2 %collective-permute-start.11 = (f32[2,64,2560]{2,1,0:T(8,128)}, f32[2,64,2560]{2,1,0:T(8,128)}, u32[]{:S(2)}, u32[]{:S(2)}) collective-permute-start(f32[2,64,2560]{2,1,0:T(8,128)} %dynamic-slice_bitcast_fusion.4), channel_id=1, source_target_pairs={{0,2},{2,0},{4,6},{6,4},{1,3},{3,1},{5,7},{7,5},{8,10},{10,8},{12,... | collective-permute-start | bytes 3932168 | tf_op jit(solution)/shard_map/ppermute | solution.py:70
  70.4 17.7 %collective-permute-start.18 = (bf16[128,2560]{1,0:T(8,128)(2,1)}, bf16[128,2560]{1,0:T(8,128)(2,1)S(1)}, u32[]{:S(2)}, u32[]{:S(2)}) collective-permute-start(bf16[128,2560]{1,0:T(8,128)(2,1)} %collective-permute-done.17), channel_id=1, source_target_pairs={{0,1},{1,0},{2,3},{3,2},{4,5},{5,4},{6,7},{7,6},{8,9},{9,8},{10,11... | collective-permute-start | bytes 1966088 | tf_op jit(solution)/shard_map/ppermute | solution.py:67
  71.9 29.9 %collective-permute-start.21 = (bf16[128,2560]{1,0:T(8,128)(2,1)}, bf16[128,2560]{1,0:T(8,128)(2,1)S(1)}, u32[]{:S(2)}, u32[]{:S(2)}) collective-permute-start(bf16[128,2560]{1,0:T(8,128)(2,1)} %collective-permute-done.20), channel_id=1, source_target_pairs={{0,1},{1,0},{2,3},{3,2},{4,5},{5,4},{6,7},{7,6},{8,9},{9,8},{10,11... | collective-permute-start | bytes 1966088 | tf_op jit(solution)/shard_map/ppermute | solution.py:67
  88.1 23.7 %collective-permute-start.28 = (bf16[128,2560]{1,0:T(8,128)(2,1)}, bf16[128,2560]{1,0:T(8,128)(2,1)}, u32[]{:S(2)}, u32[]{:S(2)}) collective-permute-start(bf16[128,2560]{1,0:T(8,128)(2,1)} %collective-permute-done.17), channel_id=1, source_target_pairs={{0,8},{8,16},{16,24},{24,0},{1,9},{9,17},{17,25},{25,1},{2,10},{10... | collective-permute-start | bytes 1966088 | tf_op jit(solution)/shard_map/ppermute | solution.py:67
  96.9 23.4 %collective-permute-start.31 = (bf16[128,2560]{1,0:T(8,128)(2,1)}, bf16[128,2560]{1,0:T(8,128)(2,1)}, u32[]{:S(2)}, u32[]{:S(2)}) collective-permute-start(bf16[128,2560]{1,0:T(8,128)(2,1)} %collective-permute-done.20), channel_id=1, source_target_pairs={{0,8},{8,16},{16,24},{24,0},{1,9},{9,17},{17,25},{25,1},{2,10},{10... | collective-permute-start | bytes 1966088 | tf_op jit(solution)/shard_map/ppermute | solution.py:67
  101.8 87.9 %collective-permute-start.3 = (bf16[64,5120]{1,0:T(8,128)(2,1)}, bf16[64,5120]{1,0:T(8,128)(2,1)}, u32[]{:S(2)}, u32[]{:S(2)}) collective-permute-start(bf16[64,5120]{1,0:T(8,128)(2,1)} %pad_maximum_fusion.11), channel_id=1, source_target_pairs={{0,4},{2,6},{4,0},{6,2},{1,5},{3,7},{5,1},{7,3},{8,12},{10,14},{12... | collective-permute-start | bytes 1966088 | tf_op jit(solution)/shard_map/ppermute | solution.py:75
  103.3 7.2 %copy-start.8 = (bf16[256,2560]{1,0:T(8,128)(2,1)}, bf16[256,2560]{1,0:T(8,128)(2,1)S(1)}, u32[]{:S(2)}) copy-start(bf16[256,2560]{1,0:T(8,128)(2,1)S(1)} %constant_dynamic-update-slice_fusion.6.refs_6_) | copy-start | bytes 3932164
  111.8 51.2 %collective-permute-start.19 = (f32[2,64,2560]{2,1,0:T(8,128)}, f32[2,64,2560]{2,1,0:T(8,128)}, u32[]{:S(2)}, u32[]{:S(2)}) collective-permute-start(f32[2,64,2560]{2,1,0:T(8,128)} %dynamic-slice_bitcast_fusion.3), channel_id=1, source_target_pairs={{0,2},{2,0},{4,6},{6,4},{1,3},{3,1},{5,7},{7,5},{8,10},{10,8},{12,... | collective-permute-start | bytes 3932168 | tf_op jit(solution)/shard_map/ppermute | solution.py:70
  120.2 45.0 %collective-permute-start.22 = (f32[2,64,2560]{2,1,0:T(8,128)}, f32[2,64,2560]{2,1,0:T(8,128)}, u32[]{:S(2)}, u32[]{:S(2)}) collective-permute-start(f32[2,64,2560]{2,1,0:T(8,128)} %dynamic-slice_bitcast_fusion.2), channel_id=1, source_target_pairs={{0,2},{2,0},{4,6},{6,4},{1,3},{3,1},{5,7},{7,5},{8,10},{10,8},{12,... | collective-permute-start | bytes 3932168 | tf_op jit(solution)/shard_map/ppermute | solution.py:70
  121.4 17.8 %collective-permute-start.29 = (bf16[128,2560]{1,0:T(8,128)(2,1)}, bf16[128,2560]{1,0:T(8,128)(2,1)S(1)}, u32[]{:S(2)}, u32[]{:S(2)}) collective-permute-start(bf16[128,2560]{1,0:T(8,128)(2,1)} %collective-permute-done.28), channel_id=1, source_target_pairs={{0,1},{1,0},{2,3},{3,2},{4,5},{5,4},{6,7},{7,6},{8,9},{9,8},{10,11... | collective-permute-start | bytes 1966088 | tf_op jit(solution)/shard_map/ppermute | solution.py:67
  124.6 28.3 %collective-permute-start.32 = (bf16[128,2560]{1,0:T(8,128)(2,1)}, bf16[128,2560]{1,0:T(8,128)(2,1)S(1)}, u32[]{:S(2)}, u32[]{:S(2)}) collective-permute-start(bf16[128,2560]{1,0:T(8,128)(2,1)} %collective-permute-done.31), channel_id=1, source_target_pairs={{0,1},{1,0},{2,3},{3,2},{4,5},{5,4},{6,7},{7,6},{8,9},{9,8},{10,11... | collective-permute-start | bytes 1966088 | tf_op jit(solution)/shard_map/ppermute | solution.py:67
  139.2 29.7 %collective-permute-start.12 = (bf16[64,5120]{1,0:T(8,128)(2,1)S(1)}, bf16[64,5120]{1,0:T(8,128)(2,1)}, u32[]{:S(2)}, u32[]{:S(2)}) collective-permute-start(bf16[64,5120]{1,0:T(8,128)(2,1)S(1)} %pad_maximum_fusion.12), channel_id=1, source_target_pairs={{0,4},{2,6},{4,0},{6,2},{1,5},{3,7},{5,1},{7,3},{8,12},{10,14},{12... | collective-permute-start | bytes 1966088 | tf_op jit(solution)/shard_map/ppermute | solution.py:75
  140.7 7.1 %copy-start.4 = (bf16[256,2560]{1,0:T(8,128)(2,1)}, bf16[256,2560]{1,0:T(8,128)(2,1)S(1)}, u32[]{:S(2)}) copy-start(bf16[256,2560]{1,0:T(8,128)(2,1)S(1)} %constant_dynamic-update-slice_fusion.8.refs_3_) | copy-start | bytes 3932164
  152.9 34.2 %collective-permute-start.30 = (f32[2,64,2560]{2,1,0:T(8,128)}, f32[2,64,2560]{2,1,0:T(8,128)S(1)}, u32[]{:S(2)}, u32[]{:S(2)}) collective-permute-start(f32[2,64,2560]{2,1,0:T(8,128)} %dynamic-slice_bitcast_fusion.1), channel_id=1, source_target_pairs={{0,2},{2,0},{4,6},{6,4},{1,3},{3,1},{5,7},{7,5},{8,10},{10,8},{12,... | collective-permute-start | bytes 3932168 | tf_op jit(solution)/shard_map/ppermute | solution.py:70
  152.9 8.7 %copy-start.2 = (bf16[256,2560]{1,0:T(8,128)(2,1)}, bf16[256,2560]{1,0:T(8,128)(2,1)S(1)}, u32[]{:S(2)}) copy-start(bf16[256,2560]{1,0:T(8,128)(2,1)S(1)} %constant_dynamic-update-slice_fusion.10.refs_7_) | copy-start | bytes 3932164
  163.0 24.3 %collective-permute-start.33 = (f32[2,64,2560]{2,1,0:T(8,128)S(1)}, f32[2,64,2560]{2,1,0:T(8,128)S(1)}, u32[]{:S(2)}, u32[]{:S(2)}) collective-permute-start(f32[2,64,2560]{2,1,0:T(8,128)S(1)} %dynamic-slice_bitcast_fusion), channel_id=1, source_target_pairs={{0,2},{2,0},{4,6},{6,4},{1,3},{3,1},{5,7},{7,5},{8,10},{10,8},{12,... | collective-permute-start | bytes 3932168 | tf_op jit(solution)/shard_map/ppermute | solution.py:70
  167.3 17.7 %collective-permute-start.23 = (bf16[64,5120]{1,0:T(8,128)(2,1)S(1)}, bf16[64,5120]{1,0:T(8,128)(2,1)S(1)}, u32[]{:S(2)}, u32[]{:S(2)}) collective-permute-start(bf16[64,5120]{1,0:T(8,128)(2,1)S(1)} %pad_maximum_fusion.14), channel_id=1, source_target_pairs={{0,4},{2,6},{4,0},{6,2},{1,5},{3,7},{5,1},{7,3},{8,12},{10,14},{12... | collective-permute-start | bytes 1966088 | tf_op jit(solution)/shard_map/ppermute | solution.py:75
  170.5 28.5 %collective-permute-start.13 = (bf16[64,5120]{1,0:T(8,128)(2,1)S(1)}, bf16[64,5120]{1,0:T(8,128)(2,1)S(1)}, u32[]{:S(2)}, u32[]{:S(2)}) collective-permute-start(bf16[64,5120]{1,0:T(8,128)(2,1)S(1)} %pad_maximum_fusion.13), channel_id=1, source_target_pairs={{0,4},{2,6},{4,0},{6,2},{1,5},{3,7},{5,1},{7,3},{8,12},{10,14},{12... | collective-permute-start | bytes 1966088 | tf_op jit(solution)/shard_map/ppermute | solution.py:75
  185.5 44.6 %collective-permute-start.24 = (bf16[64,5120]{1,0:T(8,128)(2,1)S(1)}, bf16[64,5120]{1,0:T(8,128)(2,1)S(1)}, u32[]{:S(2)}, u32[]{:S(2)}) collective-permute-start(bf16[64,5120]{1,0:T(8,128)(2,1)S(1)} %pad_maximum_fusion.15), channel_id=1, source_target_pairs={{0,4},{2,6},{4,0},{6,2},{1,5},{3,7},{5,1},{7,3},{8,12},{10,14},{12... | collective-permute-start | bytes 1966088 | tf_op jit(solution)/shard_map/ppermute | solution.py:75
  189.1 37.1 %collective-permute-start.34 = (bf16[64,5120]{1,0:T(8,128)(2,1)S(1)}, bf16[64,5120]{1,0:T(8,128)(2,1)S(1)}, u32[]{:S(2)}, u32[]{:S(2)}) collective-permute-start(bf16[64,5120]{1,0:T(8,128)(2,1)S(1)} %pad_maximum_fusion.16), channel_id=1, source_target_pairs={{0,4},{2,6},{4,0},{6,2},{1,5},{3,7},{5,1},{7,3},{8,12},{10,14},{12... | collective-permute-start | bytes 1966088 | tf_op jit(solution)/shard_map/ppermute | solution.py:75
  226.7 15.9 %collective-permute-start.35 = (bf16[64,5120]{1,0:T(8,128)(2,1)S(1)}, bf16[64,5120]{1,0:T(8,128)(2,1)S(1)}, u32[]{:S(2)}, u32[]{:S(2)}) collective-permute-start(bf16[64,5120]{1,0:T(8,128)(2,1)S(1)} %pad_maximum_fusion.17), channel_id=1, source_target_pairs={{0,4},{2,6},{4,0},{6,2},{1,5},{3,7},{5,1},{7,3},{8,12},{10,14},{12... | collective-permute-start | bytes 1966088 | tf_op jit(solution)/shard_map/ppermute | solution.py:75
  228.3 16.6 %collective-permute-start.14 = (bf16[128,5120]{1,0:T(8,128)(2,1)S(1)}, bf16[128,5120]{1,0:T(8,128)(2,1)S(1)}, u32[]{:S(2)}, u32[]{:S(2)}) collective-permute-start(bf16[128,5120]{1,0:T(8,128)(2,1)S(1)} %pad_maximum_fusion.7), channel_id=1, source_target_pairs={{0,2},{2,0},{4,6},{6,4},{1,3},{3,1},{5,7},{7,5},{8,10},{10,8},{12,... | collective-permute-start | bytes 3932168 | tf_op jit(solution)/shard_map/ppermute | solution.py:70
  229.6 28.2 %collective-permute-start.4 = (bf16[128,5120]{1,0:T(8,128)(2,1)}, bf16[128,5120]{1,0:T(8,128)(2,1)}, u32[]{:S(2)}, u32[]{:S(2)}) collective-permute-start(bf16[128,5120]{1,0:T(8,128)(2,1)} %pad_maximum_fusion.6), channel_id=1, source_target_pairs={{0,2},{2,0},{4,6},{6,4},{1,3},{3,1},{5,7},{7,5},{8,10},{10,8},{12,... | collective-permute-start | bytes 3932168 | tf_op jit(solution)/shard_map/ppermute | solution.py:70
  244.3 32.2 %collective-permute-start.25 = (bf16[128,5120]{1,0:T(8,128)(2,1)}, bf16[128,5120]{1,0:T(8,128)(2,1)}, u32[]{:S(2)}, u32[]{:S(2)}) collective-permute-start(bf16[128,5120]{1,0:T(8,128)(2,1)} %pad_maximum_fusion.8), channel_id=1, source_target_pairs={{0,2},{2,0},{4,6},{6,4},{1,3},{3,1},{5,7},{7,5},{8,10},{10,8},{12,... | collective-permute-start | bytes 3932168 | tf_op jit(solution)/shard_map/ppermute | solution.py:70
  244.4 46.8 %collective-permute-start.36 = (bf16[128,5120]{1,0:T(8,128)(2,1)S(1)}, bf16[128,5120]{1,0:T(8,128)(2,1)}, u32[]{:S(2)}, u32[]{:S(2)}) collective-permute-start(bf16[128,5120]{1,0:T(8,128)(2,1)S(1)} %pad_maximum_fusion.9), channel_id=1, source_target_pairs={{0,2},{2,0},{4,6},{6,4},{1,3},{3,1},{5,7},{7,5},{8,10},{10,8},{12,... | collective-permute-start | bytes 3932168 | tf_op jit(solution)/shard_map/ppermute | solution.py:70
  256.2 17.3 %collective-permute-start.15 = (bf16[128,2560]{1,0:T(8,128)(2,1)}, bf16[128,2560]{1,0:T(8,128)(2,1)}, u32[]{:S(2)}, u32[]{:S(2)}) collective-permute-start(bf16[128,2560]{1,0:T(8,128)(2,1)} %slice.168), channel_id=1, source_target_pairs={{0,1},{1,0},{2,3},{3,2},{4,5},{5,4},{6,7},{7,6},{8,9},{9,8},{10,11... | collective-permute-start | bytes 1966088 | tf_op jit(solution)/shard_map/ppermute | solution.py:67
  270.2 77.2 %collective-permute-start.5 = (bf16[128,2560]{1,0:T(8,128)(2,1)}, bf16[128,2560]{1,0:T(8,128)(2,1)S(1)}, u32[]{:S(2)}, u32[]{:S(2)}) collective-permute-start(bf16[128,2560]{1,0:T(8,128)(2,1)} %slice.169), channel_id=1, source_target_pairs={{0,1},{1,0},{2,3},{3,2},{4,5},{5,4},{6,7},{7,6},{8,9},{9,8},{10,11... | collective-permute-start | bytes 1966088 | tf_op jit(solution)/shard_map/ppermute | solution.py:67
  276.0 71.4 %collective-permute-start.16 = (bf16[128,2560]{1,0:T(8,128)(2,1)}, bf16[128,2560]{1,0:T(8,128)(2,1)}, u32[]{:S(2)}, u32[]{:S(2)}) collective-permute-start(bf16[128,2560]{1,0:T(8,128)(2,1)} %fusion.6), channel_id=1, source_target_pairs={{0,24},{8,0},{16,8},{24,16},{1,25},{9,1},{17,9},{25,17},{2,26},{10... | collective-permute-start | bytes 1966088 | tf_op jit(solution)/shard_map/ppermute | solution.py:67
  289.0 37.1 %collective-permute-start.26 = (bf16[128,2560]{1,0:T(8,128)(2,1)}, bf16[128,2560]{1,0:T(8,128)(2,1)}, u32[]{:S(2)}, u32[]{:S(2)}) collective-permute-start(bf16[128,2560]{1,0:T(8,128)(2,1)} %slice.167), channel_id=1, source_target_pairs={{0,1},{1,0},{2,3},{3,2},{4,5},{5,4},{6,7},{7,6},{8,9},{9,8},{10,11... | collective-permute-start | bytes 1966088 | tf_op jit(solution)/shard_map/ppermute | solution.py:67
  302.9 25.5 %collective-permute-start.37 = (bf16[128,2560]{1,0:T(8,128)(2,1)S(1)}, bf16[128,2560]{1,0:T(8,128)(2,1)S(1)}, u32[]{:S(2)}, u32[]{:S(2)}) collective-permute-start(bf16[128,2560]{1,0:T(8,128)(2,1)S(1)} %slice.166), channel_id=1, source_target_pairs={{0,1},{1,0},{2,3},{3,2},{4,5},{5,4},{6,7},{7,6},{8,9},{9,8},{10,11... | collective-permute-start | bytes 1966088 | tf_op jit(solution)/shard_map/ppermute | solution.py:67
  308.2 17.9 %copy-start.20 = (f32[256,2560]{1,0:T(8,128)S(1)}, f32[256,2560]{1,0:T(8,128)}, u32[]{:S(2)}) copy-start(f32[256,2560]{1,0:T(8,128)} %fusion.4) | copy-start | bytes 7864324
  308.2 20.1 %copy-start.21 = (f32[256,2560]{1,0:T(8,128)S(1)}, f32[256,2560]{1,0:T(8,128)}, u32[]{:S(2)}) copy-start(f32[256,2560]{1,0:T(8,128)} %fusion.1) | copy-start | bytes 7864324
  327.5 43.6 %collective-permute-start.27 = (bf16[128,2560]{1,0:T(8,128)(2,1)S(1)}, bf16[128,2560]{1,0:T(8,128)(2,1)S(1)}, u32[]{:S(2)}, u32[]{:S(2)}) collective-permute-start(bf16[128,2560]{1,0:T(8,128)(2,1)S(1)} %fusion.3), channel_id=1, source_target_pairs={{0,16},{8,24},{16,0},{24,8},{1,17},{9,25},{17,1},{25,9},{2,18},{10... | collective-permute-start | bytes 1966088 | tf_op jit(solution)/shard_map/ppermute | solution.py:67
  328.5 42.6 %copy-start.22 = (f32[256,2560]{1,0:T(8,128)S(1)}, f32[256,2560]{1,0:T(8,128)}, u32[]{:S(2)}) copy-start(f32[256,2560]{1,0:T(8,128)} %fusion.13) | copy-start | bytes 7864324
  328.5 42.6 %collective-permute-start.38 = (bf16[128,2560]{1,0:T(8,128)(2,1)S(1)}, bf16[128,2560]{1,0:T(8,128)(2,1)S(1)}, u32[]{:S(2)}, u32[]{:S(2)}) collective-permute-start(bf16[128,2560]{1,0:T(8,128)(2,1)S(1)} %fusion), channel_id=1, source_target_pairs={{0,8},{8,16},{16,24},{24,0},{1,9},{9,17},{17,25},{25,1},{2,10},{10... | collective-permute-start | bytes 1966088 | tf_op jit(solution)/shard_map/ppermute | solution.py:67
  (15 other events, 34.8 us)

commit v3 on v2

--- a/solution.py
+++ b/solution.py
@@ -132,14 +132,21 @@
         halves = [a.reshape(outer, 1, shard // C, -1) for a in in_order(halves, ci)]
         return jnp.concatenate(halves, axis=1).reshape(shard, -1)
 
-    both, result = [], None
+    shares, both, result = [], [], None
     for k in range(T):
-        pre = jnp.dot(toks[k], weight_in, preferred_element_type=f32)
+        tok = toks[k]
+        if k >= 2:
+            tok, shares[k - 2] = lax.optimization_barrier((tok, shares[k - 2]))
+        pre = jnp.dot(tok, weight_in, preferred_element_type=f32)
         grad = lax.dot_general(
             grads[k], weight_out, (((1,), (1,)), ((), ())), preferred_element_type=f32
         )
-        share = jnp.concatenate(gelu_parts(*con_sum(pre, grad)), axis=1)
-        chunk = con_gather(share)
+        shares.append(jnp.concatenate(gelu_parts(*con_sum(pre, grad)), axis=1))
+    for k in range(T):
+        if k < T - 1:
+            chunk = lax.all_gather(shares[k], "con", axis=0, tiled=True)
+        else:
+            chunk = con_gather(shares[k])
         both.append(chunk)
         back = lax.dot_general(
             chunk[:, hidden:], weight_in, (((1,), (1,)), ((), ())), preferred_element_type=f32

time: 375 us -> 376 us (level)
  between operations: 1.38 us -> 14.6 us
  local copies, waits for them, and re-layouts: 37.5 us -> 45.6 us
  waiting for transfers between devices: 136 us -> 130 us
  other arithmetic: 37.4 us -> 32.1 us
  matrix products: 90.7 us -> 85.6 us
  starting transfers between devices: 35 us -> 31 us
    ppermute x8 -> x5, waiting for transfers between devices: 61.3 us -> 42.7 us  [shift_outer(): lax.ppermute(a, 'con', [(i, (i // inner + by) % outer * inner + i % inner...]
    ppermute x19, waiting for transfers between devices: 74.2 us -> 86.8 us  [shift(): return lax.ppermute(a, axis, [(i, (i + by) % size) for i in range(size)])]
    unnamed x54 -> x92, local copies, waits for them, and re-layouts: 15.8 us -> 25.2 us
    slice x4, local copies, waits for them, and re-layouts: 8.04 us -> 2.03 us  [per_device(): sent = back[j * rows:(j + 1) * rows].astype(bf16)]
    select_n x6 -> x2, other arithmetic: 8.23 us -> 2.23 us  [in_order(): block = jnp.where(k == other, blocks[other], block)]
    dot_general x4, matrix products: 32.9 us -> 28.2 us  [per_device(): lax.dot_general(chunk[:, hidden:], weight_in, (((1,), (1,)), ((), ())), p...]
    concatenate x6, local copies, waits for them, and re-layouts: 0.26 us -> 4.61 us  [whole_shard(): jnp.concatenate([own] + [shift(own, 'out', O, k) for k in range(1, O)], a...]
    ppermute x8 -> x5, starting transfers between devices: 10.4 us -> 6.99 us  [shift_outer(): lax.ppermute(a, 'con', [(i, (i // inner + by) % outer * inner + i % inner...]
  transfers between devices with their start and end apart: 39 -> 36, of which waited for: 14 -> 12; matrix products, arithmetic and copies ran while one was open for 41% -> 37% of each run, Pallas kernels for 10% -> 10%
where the time goes in v3:
time: 376 us; the launch traced here: 374 us
  waiting for transfers between devices  130 us (35%)
  matrix products  85.6 us (23%)
  local copies, waits for them, and re-layouts  45.6 us (12%)
  Pallas kernels  35.9 us (10%)
  other arithmetic  32.1 us (9%)
  starting transfers between devices  31 us (8%)
  between operations  14.6 us (4%)
    ppermute x19, waiting for transfers between devices, shift(): return lax.ppermute(a, axis, [(i, (i + by) % size) for i in range(size)])  86.8 us
    ppermute x5, waiting for transfers between devices, shift_outer(): lax.ppermute(a, 'con', [(i, (i // inner + by) % outer * inner + i % inner...  42.7 us
    pallas_call x2, Pallas kernels, summed_outer(): pl.pallas_call(functools.partial(grad_kernel, chunks, width), grid=(left_...  35.9 us
    dot_general x4, matrix products, per_device(): lax.dot_general(grads[k], weight_out, (((1,), (1,)), ((), ())), preferred...  29.8 us
    dot_general x4, matrix products, per_device(): lax.dot_general(chunk[:, hidden:], weight_in, (((1,), (1,)), ((), ())), p...  28.2 us
    dot_general x4, matrix products, per_device(): pre = jnp.dot(tok, weight_in, preferred_element_type=f32)  27.6 us
    unnamed x92, local copies, waits for them, and re-layouts  25.2 us
    ppermute x19, starting transfers between devices, shift(): return lax.ppermute(a, axis, [(i, (i + by) % size) for i in range(size)])  22.5 us
  transfers between devices with their start and end apart: 36, of which 12 were waited for; matrix products, arithmetic and copies ran while one was open for 37% of the time, Pallas kernels for 10%

profile of v3, /device:TPU:0, one launch (start us, length us, event | category | flops | bytes accessed | tf_op | source)
XLA Modules:
  0.0 374.3 jit_solution(12138178476457002146)
XLA Ops:
  7.2 2.2 constant_dynamic-slice_fusion.2
  9.5 3.0 collective-permute-start
  12.5 6.8 %fusion.48 = f32[256,2560]{1,0:T(8,128)S(1)} fusion(bf16[2560,2560]{1,0:T(8,128)(2,1)} %param.6, bf16[128,2560]{1,0:T(8,128)(2,1)S(1)} %get-tuple-element.23, bf16[128,2560]{1,0:T(8,128)(2,1)} %get-tuple-element.24), kind=kOutput, calls=%fused_computation.132 | convolution fusion | flops 3358064640 | bytes 17039360 | tf_op jit(solution)/shard_map/dot_general | solution.py:140
  22.0 1.6 collective-permute-start.11
  23.6 6.8 %fusion.47 = f32[256,2560]{1,0:T(8,128)S(1)} fusion(bf16[2560,2560]{1,0:T(8,128)(2,1)} %param.7, bf16[128,2560]{1,0:T(8,128)(2,1)S(1)} %get-tuple-element.26, bf16[128,2560]{1,0:T(8,128)(2,1)} %get-tuple-element.25), kind=kOutput, calls=%fused_computation.131 | convolution fusion | flops 3358064640 | bytes 17039360 | tf_op jit(solution)/shard_map/dot_general | solution.py:141
  32.4 11.2 %collective-permute-done.11 = bf16[128,2560]{1,0:T(8,128)(2,1)} collective-permute-done((bf16[128,2560]{1,0:T(8,128)(2,1)}, bf16[128,2560]{1,0:T(8,128)(2,1)}, u32[]{:S(2)}, u32[]{:S(2)}) %collective-permute-start.11) | collective-permute-done | bytes 655392 | tf_op jit(solution)/shard_map/ppermute | solution.py:67
  43.6 1.5 collective-permute-start.12
  49.3 1.6 bitcast_add_fusion.7
  51.4 1.5 bitcast_add_fusion.6
  53.0 1.6 collective-permute-start.5
  54.5 7.0 %collective-permute-done.12 = bf16[128,2560]{1,0:T(8,128)(2,1)S(1)} collective-permute-done((bf16[128,2560]{1,0:T(8,128)(2,1)}, bf16[128,2560]{1,0:T(8,128)(2,1)S(1)}, u32[]{:S(2)}, u32[]{:S(2)}) %collective-permute-start.12) | collective-permute-done | bytes 655392 | tf_op jit(solution)/shard_map/ppermute | solution.py:67
  61.5 7.1 %fusion.50 = f32[256,2560]{1,0:T(8,128)S(1)} fusion(bf16[256,2560]{1,0:T(8,128)(2,1)S(1)} %constant_dynamic-update-slice_fusion.6.refs_5_, bf16[2560,2560]{1,0:T(8,128)(2,1)} %param.7), kind=kOutput, calls=%fused_computation.134 | convolution fusion | flops 3355443200 | bytes 17039360 | tf_op jit(solution)/shard_map/dot_general | solution.py:141
  70.6 3.3 collective-permute-done.9
  75.0 7.1 %fusion.49 = f32[256,2560]{1,0:T(8,128)S(1)} fusion(bf16[256,2560]{1,0:T(8,128)(2,1)S(1)} %constant_dynamic-update-slice_fusion.4.refs_1_, bf16[2560,2560]{1,0:T(8,128)(2,1)} %param.6), kind=kOutput, calls=%fused_computation.133 | convolution fusion | flops 3355443200 | bytes 17039360 | tf_op jit(solution)/shard_map/dot_general | solution.py:140
  91.6 10.3 %collective-permute-done.2 = bf16[128,2560]{1,0:T(8,128)(2,1)} collective-permute-done((bf16[128,2560]{1,0:T(8,128)(2,1)}, bf16[128,2560]{1,0:T(8,128)(2,1)}, u32[]{:S(2)}, u32[]{:S(2)}) %collective-permute-start.2) | collective-permute-done | bytes 655392 | tf_op jit(solution)/shard_map/ppermute | solution.py:67
  103.8 7.1 %fusion.51 = f32[256,2560]{1,0:T(8,128)S(1)} fusion(bf16[256,2560]{1,0:T(8,128)(2,1)S(1)} %constant_dynamic-update-slice_fusion.refs_2_, bf16[2560,2560]{1,0:T(8,128)(2,1)} %param.6), kind=kOutput, calls=%fused_computation.135 | convolution fusion | flops 3355443200 | bytes 17039360 | tf_op jit(solution)/shard_map/dot_general | solution.py:140
  112.8 2.8 collective-permute-done.19
  116.7 8.6 %fusion.52 = f32[256,2560]{1,0:T(8,128)} fusion(bf16[256,2560]{1,0:T(8,128)(2,1)S(1)} %constant_dynamic-update-slice_fusion.8.refs_6_, bf16[2560,2560]{1,0:T(8,128)(2,1)} %param.7), kind=kOutput, calls=%fused_computation.136 | convolution fusion | flops 3355443200 | bytes 17039360 | tf_op jit(solution)/shard_map/dot_general | solution.py:141
  125.7 2.7 dynamic-slice_bitcast_fusion.2
  133.3 1.7 bitcast_add_fusion.4
  138.5 22.4 %collective-permute-done.26 = bf16[128,2560]{1,0:T(8,128)(2,1)S(1)} collective-permute-done((bf16[128,2560]{1,0:T(8,128)(2,1)}, bf16[128,2560]{1,0:T(8,128)(2,1)S(1)}, u32[]{:S(2)}, u32[]{:S(2)}) %collective-permute-start.26) | collective-permute-done | bytes 655392 | tf_op jit(solution)/shard_map/ppermute | solution.py:67
  161.0 7.2 %fusion.54 = f32[256,2560]{1,0:T(8,128)S(1)} fusion(bf16[256,2560]{1,0:T(8,128)(2,1)S(1)} %constant_dynamic-update-slice_fusion.10.refs_7_, bf16[2560,2560]{1,0:T(8,128)(2,1)} %param.7), kind=kOutput, calls=%fused_computation.138 | convolution fusion | flops 3355443200 | bytes 17039360 | tf_op jit(solution)/shard_map/dot_general | solution.py:141
  172.6 6.6 %fusion.53 = f32[256,2560]{1,0:T(8,128)S(1)} fusion(bf16[256,2560]{1,0:T(8,128)(2,1)S(1)} %constant_dynamic-update-slice_fusion.2.refs_3_, bf16[2560,2560]{1,0:T(8,128)(2,1)} %param.6), kind=kOutput, calls=%fused_computation.137 | convolution fusion | flops 3355443200 | bytes 17039360 | tf_op jit(solution)/shard_map/dot_general | solution.py:140
  181.8 1.5 bitcast_add_fusion.2
  185.6 1.5 bitcast_add_fusion
  191.1 2.3 pad_maximum_fusion.2.refs_4_
  193.4 2.3 pad_maximum_fusion.1.refs_0_
  195.7 6.5 %collective-permute-done.21 = bf16[64,5120]{1,0:T(8,128)(2,1)} collective-permute-done((bf16[64,5120]{1,0:T(8,128)(2,1)}, bf16[64,5120]{1,0:T(8,128)(2,1)}, u32[]{:S(2)}, u32[]{:S(2)}) %collective-permute-start.21) | collective-permute-done | bytes 655392 | tf_op jit(solution)/shard_map/ppermute | solution.py:75
  203.6 21.8 %collective-permute-done.28 = bf16[64,5120]{1,0:T(8,128)(2,1)} collective-permute-done((bf16[64,5120]{1,0:T(8,128)(2,1)}, bf16[64,5120]{1,0:T(8,128)(2,1)}, u32[]{:S(2)}, u32[]{:S(2)}) %collective-permute-start.28) | collective-permute-done | bytes 655392 | tf_op jit(solution)/shard_map/ppermute | solution.py:75
  227.0 2.2 collective-permute-start.29
  229.5 14.3 %collective-permute-done.29 = bf16[64,5120]{1,0:T(8,128)(2,1)S(1)} collective-permute-done((bf16[64,5120]{1,0:T(8,128)(2,1)S(1)}, bf16[64,5120]{1,0:T(8,128)(2,1)S(1)}, u32[]{:S(2)}, u32[]{:S(2)}) %collective-permute-start.29) | collective-permute-done | bytes 655392 | tf_op jit(solution)/shard_map/ppermute | solution.py:75
  245.2 7.0 %fusion.13 = f32[256,2560]{1,0:T(8,128)S(1)} fusion(bf16[2560,2560]{1,0:T(8,128)(2,1)} %param.6, bf16[256,5120]{1,0:T(8,128)(2,1)} %all-gather.4.cloned.1.call-done.refs_4_.refs_0_), kind=kOutput, calls=%fused_computation.22 | convolution fusion | flops 3355443200 | bytes 17039360 | tf_op jit(solution)/shard_map/dot_general | solution.py:151
  254.5 2.0 broadcast_select_fusion.1
  256.8 6.7 %fusion.1 = f32[256,2560]{1,0:T(8,128)S(1)} fusion(bf16[2560,2560]{1,0:T(8,128)(2,1)} %param.6, bf16[256,5120]{1,0:T(8,128)(2,1)S(1)} %bitcast.145), kind=kOutput, calls=%fused_computation.4 | convolution fusion | flops 3355443200 | bytes 17039360 | tf_op jit(solution)/shard_map/dot_general | solution.py:151
  263.5 1.5 copy-done.36
  266.7 7.2 %fusion.7 = f32[256,2560]{1,0:T(8,128)S(1)} fusion(bf16[2560,2560]{1,0:T(8,128)(2,1)} %param.6, bf16[256,5120]{1,0:T(8,128)(2,1)} %all-gather.6.cloned.1.call-done.refs_5_.refs_1_), kind=kOutput, calls=%fused_computation.14 | convolution fusion | flops 3355443200 | bytes 17039360 | tf_op jit(solution)/shard_map/dot_general | solution.py:151
  275.3 9.8 %collective-permute-done.31 = bf16[128,2560]{1,0:T(8,128)(2,1)} collective-permute-done((bf16[128,2560]{1,0:T(8,128)(2,1)}, bf16[128,2560]{1,0:T(8,128)(2,1)}, u32[]{:S(2)}, u32[]{:S(2)}) %collective-permute-start.31) | collective-permute-done | bytes 655392 | tf_op jit(solution)/shard_map/ppermute | solution.py:67
  285.1 2.1 fusion
  287.9 10.8 %collective-permute-done.15 = bf16[128,2560]{1,0:T(8,128)(2,1)S(1)} collective-permute-done((bf16[128,2560]{1,0:T(8,128)(2,1)S(1)}, bf16[128,2560]{1,0:T(8,128)(2,1)S(1)}, u32[]{:S(2)}, u32[]{:S(2)}) %collective-permute-start.15) | collective-permute-done | bytes 655392 | tf_op jit(solution)/shard_map/ppermute | solution.py:67
  299.7 3.5 collective-permute-start.16
  303.2 7.2 %fusion.4 = f32[256,2560]{1,0:T(8,128)S(1)} fusion(bf16[2560,2560]{1,0:T(8,128)(2,1)} %param.6, bf16[256,5120]{1,0:T(8,128)(2,1)} %all-gather.8.cloned.1.call-done.refs_6_.refs_2_), kind=kOutput, calls=%fused_computation.9 | convolution fusion | flops 3355443200 | bytes 17039360 | tf_op jit(solution)/shard_map/dot_general | solution.py:151
  313.2 1.7 copy-done.14
  314.9 1.7 copy-done.16
  316.7 1.7 copy-done.18
  318.4 17.9 %shard_map.68 = f32[2560,2560]{1,0:T(8,128)} custom-call(bf16[256,5120]{1,0:T(8,128)(2,1)S(1)} %copy-done.14, bf16[256,5120]{1,0:T(8,128)(2,1)S(1)} %copy-done.16, bf16[256,5120]{1,0:T(8,128)(2,1)S(1)} %copy-done.18, bf16[256,5120]{1,0:T(8,128)(2,1)S(1)} %bitcast.146, bf16[256,2560]{1,0:T(8,128)(2,1)S(1)} %copy-done.1, bf16[256,2560]{1,0:T(8,128)(2,1)S(1)} %copy-done.9, ...), custom_call_target="tpu_custom_call" | custom-call | flops 13421772800 | bytes 36700160 | tf_op jit(solution)/shard_map/pallas_call | solution.py:40
  338.0 18.0 %shard_map.67 = f32[2560,2560]{1,0:T(8,128)} custom-call(bf16[256,2560]{1,0:T(8,128)(2,1)S(1)} %copy-done, bf16[256,2560]{1,0:T(8,128)(2,1)S(1)} %copy-done.5, bf16[256,2560]{1,0:T(8,128)(2,1)S(1)} %copy-done.11, bf16[256,2560]{1,0:T(8,128)(2,1)S(1)} %copy-done.3, bf16[256,5120]{1,0:T(8,128)(2,1)S(1)} %copy-done.15, bf16[256,5120]{1,0:T(8,128)(2,1)S(1)} %copy-done.17, ...), custom_call_target="tpu_custom_call" | custom-call | flops 13421772800 | bytes 36700160 | tf_op jit(solution)/shard_map/pallas_call | solution.py:40
  356.1 9.3 %collective-permute-done.23 = bf16[128,2560]{1,0:T(8,128)(2,1)S(1)} collective-permute-done((bf16[128,2560]{1,0:T(8,128)(2,1)S(1)}, bf16[128,2560]{1,0:T(8,128)(2,1)S(1)}, u32[]{:S(2)}, u32[]{:S(2)}) %collective-permute-start.23) | collective-permute-done | bytes 655392 | tf_op jit(solution)/shard_map/ppermute | solution.py:67
  365.3 2.5 fusion.12
  (195 shorter events, 65.0 us)
Async XLA Ops:
  7.2 238.0 %all-gather.4.cloned.1.call-start = ((), (), s32[]{:S(2)}) async-start(), calls=%async_computation | async-start | bytes 3276800 | tf_op jit(solution)/shard_map/all_gather | solution.py:147
  9.5 35.7 %collective-permute-start = (bf16[128,2560]{1,0:T(8,128)(2,1)}, bf16[128,2560]{1,0:T(8,128)(2,1)}, u32[]{:S(2)}, u32[]{:S(2)}) collective-permute-start(bf16[128,2560]{1,0:T(8,128)(2,1)} %get-tuple-element.24), channel_id=1, source_target_pairs={{0,8},{8,16},{16,24},{24,0},{1,9},{9,17},{17,25},{25,1},{2,10},{10... | collective-permute-start | bytes 1966088 | tf_op jit(solution)/shard_map/ppermute | solution.py:67
  20.5 28.2 %collective-permute-start.3 = (f32[2,64,2560]{2,1,0:T(8,128)}, f32[2,64,2560]{2,1,0:T(8,128)}, u32[]{:S(2)}, u32[]{:S(2)}) collective-permute-start(f32[2,64,2560]{2,1,0:T(8,128)} %dynamic-slice_bitcast_fusion.7), channel_id=1, source_target_pairs={{0,2},{2,0},{4,6},{6,4},{1,3},{3,1},{5,7},{7,5},{8,10},{10,8},{12,... | collective-permute-start | bytes 3932168 | tf_op jit(solution)/shard_map/ppermute | solution.py:70
  22.0 21.6 %collective-permute-start.11 = (bf16[128,2560]{1,0:T(8,128)(2,1)}, bf16[128,2560]{1,0:T(8,128)(2,1)}, u32[]{:S(2)}, u32[]{:S(2)}) collective-permute-start(bf16[128,2560]{1,0:T(8,128)(2,1)} %get-tuple-element.25), channel_id=1, source_target_pairs={{0,8},{8,16},{16,24},{24,0},{1,9},{9,17},{17,25},{25,1},{2,10},{10... | collective-permute-start | bytes 1966088 | tf_op jit(solution)/shard_map/ppermute | solution.py:67
  32.4 18.6 %collective-permute-start.4 = (f32[2,64,2560]{2,1,0:T(8,128)}, f32[2,64,2560]{2,1,0:T(8,128)}, u32[]{:S(2)}, u32[]{:S(2)}) collective-permute-start(f32[2,64,2560]{2,1,0:T(8,128)} %dynamic-slice_bitcast_fusion.6), channel_id=1, source_target_pairs={{0,2},{2,0},{4,6},{6,4},{1,3},{3,1},{5,7},{7,5},{8,10},{10,8},{12,... | collective-permute-start | bytes 3932168 | tf_op jit(solution)/shard_map/ppermute | solution.py:70
  43.6 41.8 %collective-permute-start.18 = (bf16[128,2560]{1,0:T(8,128)(2,1)}, bf16[128,2560]{1,0:T(8,128)(2,1)}, u32[]{:S(2)}, u32[]{:S(2)}) collective-permute-start(bf16[128,2560]{1,0:T(8,128)(2,1)} %collective-permute-done.11), channel_id=1, source_target_pairs={{0,8},{8,16},{16,24},{24,0},{1,9},{9,17},{17,25},{25,1},{2,10},{10... | collective-permute-start | bytes 1966088 | tf_op jit(solution)/shard_map/ppermute | solution.py:67
  43.6 17.9 %collective-permute-start.12 = (bf16[128,2560]{1,0:T(8,128)(2,1)}, bf16[128,2560]{1,0:T(8,128)(2,1)S(1)}, u32[]{:S(2)}, u32[]{:S(2)}) collective-permute-start(bf16[128,2560]{1,0:T(8,128)(2,1)} %collective-permute-done.11), channel_id=1, source_target_pairs={{0,1},{1,0},{2,3},{3,2},{4,5},{5,4},{6,7},{7,6},{8,9},{9,8},{10,11... | collective-permute-start | bytes 1966088 | tf_op jit(solution)/shard_map/ppermute | solution.py:67
  45.1 38.9 %collective-permute-start.1 = (bf16[128,2560]{1,0:T(8,128)(2,1)}, bf16[128,2560]{1,0:T(8,128)(2,1)}, u32[]{:S(2)}, u32[]{:S(2)}) collective-permute-start(bf16[128,2560]{1,0:T(8,128)(2,1)} %collective-permute-done), channel_id=1, source_target_pairs={{0,8},{8,16},{16,24},{24,0},{1,9},{9,17},{17,25},{25,1},{2,10},{10... | collective-permute-start | bytes 1966088 | tf_op jit(solution)/shard_map/ppermute | solution.py:67
  48.7 25.2 %collective-permute-start.9 = (bf16[128,2560]{1,0:T(8,128)(2,1)}, bf16[128,2560]{1,0:T(8,128)(2,1)}, u32[]{:S(2)}, u32[]{:S(2)}) collective-permute-start(bf16[128,2560]{1,0:T(8,128)(2,1)} %collective-permute-done), channel_id=1, source_target_pairs={{0,1},{1,0},{2,3},{3,2},{4,5},{5,4},{6,7},{7,6},{8,9},{9,8},{10,11... | collective-permute-start | bytes 1966088 | tf_op jit(solution)/shard_map/ppermute | solution.py:67
  53.0 35.4 %collective-permute-start.5 = (bf16[64,5120]{1,0:T(8,128)(2,1)S(1)}, bf16[64,5120]{1,0:T(8,128)(2,1)}, u32[]{:S(2)}, u32[]{:S(2)}) collective-permute-start(bf16[64,5120]{1,0:T(8,128)(2,1)S(1)} %pad_maximum_fusion.4), channel_id=1, source_target_pairs={{0,4},{2,6},{4,0},{6,2},{1,5},{3,7},{5,1},{7,3},{8,12},{10,14},{12... | collective-permute-start | bytes 1966088 | tf_op jit(solution)/shard_map/ppermute | solution.py:75
  70.6 61.8 %collective-permute-start.13 = (f32[2,64,2560]{2,1,0:T(8,128)}, f32[2,64,2560]{2,1,0:T(8,128)}, u32[]{:S(2)}, u32[]{:S(2)}) collective-permute-start(f32[2,64,2560]{2,1,0:T(8,128)} %dynamic-slice_bitcast_fusion.4), channel_id=1, source_target_pairs={{0,2},{2,0},{4,6},{6,4},{1,3},{3,1},{5,7},{7,5},{8,10},{10,8},{12,... | collective-permute-start | bytes 3932168 | tf_op jit(solution)/shard_map/ppermute | solution.py:70
  84.1 50.9 %collective-permute-start.10 = (f32[2,64,2560]{2,1,0:T(8,128)}, f32[2,64,2560]{2,1,0:T(8,128)}, u32[]{:S(2)}, u32[]{:S(2)}) collective-permute-start(f32[2,64,2560]{2,1,0:T(8,128)} %dynamic-slice_bitcast_fusion.5), channel_id=1, source_target_pairs={{0,2},{2,0},{4,6},{6,4},{1,3},{3,1},{5,7},{7,5},{8,10},{10,8},{12,... | collective-permute-start | bytes 3932168 | tf_op jit(solution)/shard_map/ppermute | solution.py:70
  84.1 17.8 %collective-permute-start.2 = (bf16[128,2560]{1,0:T(8,128)(2,1)}, bf16[128,2560]{1,0:T(8,128)(2,1)}, u32[]{:S(2)}, u32[]{:S(2)}) collective-permute-start(bf16[128,2560]{1,0:T(8,128)(2,1)} %collective-permute-done.1), channel_id=1, source_target_pairs={{0,1},{1,0},{2,3},{3,2},{4,5},{5,4},{6,7},{7,6},{8,9},{9,8},{10,11... | collective-permute-start | bytes 1966088 | tf_op jit(solution)/shard_map/ppermute | solution.py:67
  85.4 30.2 %collective-permute-start.19 = (bf16[128,2560]{1,0:T(8,128)(2,1)}, bf16[128,2560]{1,0:T(8,128)(2,1)}, u32[]{:S(2)}, u32[]{:S(2)}) collective-permute-start(bf16[128,2560]{1,0:T(8,128)(2,1)} %collective-permute-done.18), channel_id=1, source_target_pairs={{0,1},{1,0},{2,3},{3,2},{4,5},{5,4},{6,7},{7,6},{8,9},{9,8},{10,11... | collective-permute-start | bytes 1966088 | tf_op jit(solution)/shard_map/ppermute | solution.py:67
  88.4 39.9 %collective-permute-start.7 = (bf16[128,2560]{1,0:T(8,128)(2,1)}, bf16[128,2560]{1,0:T(8,128)(2,1)}, u32[]{:S(2)}, u32[]{:S(2)}) collective-permute-start(bf16[128,2560]{1,0:T(8,128)(2,1)} %collective-permute-done.1), channel_id=1, source_target_pairs={{0,8},{8,16},{16,24},{24,0},{1,9},{9,17},{17,25},{25,1},{2,10},{10... | collective-permute-start | bytes 1966088 | tf_op jit(solution)/shard_map/ppermute | solution.py:67
  101.9 28.0 %collective-permute-start.25 = (bf16[128,2560]{1,0:T(8,128)(2,1)}, bf16[128,2560]{1,0:T(8,128)(2,1)}, u32[]{:S(2)}, u32[]{:S(2)}) collective-permute-start(bf16[128,2560]{1,0:T(8,128)(2,1)} %collective-permute-done.18), channel_id=1, source_target_pairs={{0,8},{8,16},{16,24},{24,0},{1,9},{9,17},{17,25},{25,1},{2,10},{10... | collective-permute-start | bytes 1966088 | tf_op jit(solution)/shard_map/ppermute | solution.py:67
  115.6 64.4 %collective-permute-start.17 = (f32[2,64,2560]{2,1,0:T(8,128)}, f32[2,64,2560]{2,1,0:T(8,128)S(1)}, u32[]{:S(2)}, u32[]{:S(2)}) collective-permute-start(f32[2,64,2560]{2,1,0:T(8,128)} %dynamic-slice_bitcast_fusion.3), channel_id=1, source_target_pairs={{0,2},{2,0},{4,6},{6,4},{1,3},{3,1},{5,7},{7,5},{8,10},{10,8},{12,... | collective-permute-start | bytes 3932168 | tf_op jit(solution)/shard_map/ppermute | solution.py:70
  125.4 141.3 %all-gather.6.cloned.1.call-start = ((), (), s32[]{:S(2)}) async-start(), calls=%async_computation.1 | async-start | bytes 3276800 | tf_op jit(solution)/shard_map/all_gather | solution.py:147
  128.3 52.9 %collective-permute-start.20 = (f32[2,64,2560]{2,1,0:T(8,128)}, f32[2,64,2560]{2,1,0:T(8,128)}, u32[]{:S(2)}, u32[]{:S(2)}) collective-permute-start(f32[2,64,2560]{2,1,0:T(8,128)} %dynamic-slice_bitcast_fusion.2), channel_id=1, source_target_pairs={{0,2},{2,0},{4,6},{6,4},{1,3},{3,1},{5,7},{7,5},{8,10},{10,8},{12,... | collective-permute-start | bytes 3932168 | tf_op jit(solution)/shard_map/ppermute | solution.py:70
  130.0 40.1 %collective-permute-start.8 = (bf16[128,2560]{1,0:T(8,128)(2,1)}, bf16[128,2560]{1,0:T(8,128)(2,1)}, u32[]{:S(2)}, u32[]{:S(2)}) collective-permute-start(bf16[128,2560]{1,0:T(8,128)(2,1)} %collective-permute-done.7), channel_id=1, source_target_pairs={{0,1},{1,0},{2,3},{3,2},{4,5},{5,4},{6,7},{7,6},{8,9},{9,8},{10,11... | collective-permute-start | bytes 1966088 | tf_op jit(solution)/shard_map/ppermute | solution.py:67
  132.5 28.5 %collective-permute-start.26 = (bf16[128,2560]{1,0:T(8,128)(2,1)}, bf16[128,2560]{1,0:T(8,128)(2,1)S(1)}, u32[]{:S(2)}, u32[]{:S(2)}) collective-permute-start(bf16[128,2560]{1,0:T(8,128)(2,1)} %collective-permute-done.25), channel_id=1, source_target_pairs={{0,1},{1,0},{2,3},{3,2},{4,5},{5,4},{6,7},{7,6},{8,9},{9,8},{10,11... | collective-permute-start | bytes 1966088 | tf_op jit(solution)/shard_map/ppermute | solution.py:67
  137.5 33.8 %collective-permute-start.14 = (bf16[64,5120]{1,0:T(8,128)(2,1)S(1)}, bf16[64,5120]{1,0:T(8,128)(2,1)S(1)}, u32[]{:S(2)}, u32[]{:S(2)}) collective-permute-start(bf16[64,5120]{1,0:T(8,128)(2,1)S(1)} %pad_maximum_fusion.6), channel_id=1, source_target_pairs={{0,4},{2,6},{4,0},{6,2},{1,5},{3,7},{5,1},{7,3},{8,12},{10,14},{12... | collective-permute-start | bytes 1966088 | tf_op jit(solution)/shard_map/ppermute | solution.py:75
  170.1 15.5 %collective-permute-start.27 = (f32[2,64,2560]{2,1,0:T(8,128)}, f32[2,64,2560]{2,1,0:T(8,128)}, u32[]{:S(2)}, u32[]{:S(2)}) collective-permute-start(f32[2,64,2560]{2,1,0:T(8,128)} %dynamic-slice_bitcast_fusion), channel_id=1, source_target_pairs={{0,2},{2,0},{4,6},{6,4},{1,3},{3,1},{5,7},{7,5},{8,10},{10,8},{12,... | collective-permute-start | bytes 3932168 | tf_op jit(solution)/shard_map/ppermute | solution.py:70
  179.4 7.8 %collective-permute-start.24 = (f32[2,64,2560]{2,1,0:T(8,128)S(1)}, f32[2,64,2560]{2,1,0:T(8,128)S(1)}, u32[]{:S(2)}, u32[]{:S(2)}) collective-permute-start(f32[2,64,2560]{2,1,0:T(8,128)S(1)} %dynamic-slice_bitcast_fusion.1), channel_id=1, source_target_pairs={{0,2},{2,0},{4,6},{6,4},{1,3},{3,1},{5,7},{7,5},{8,10},{10,8},{12,... | collective-permute-start | bytes 3932168 | tf_op jit(solution)/shard_map/ppermute | solution.py:70
  184.4 17.8 %collective-permute-start.21 = (bf16[64,5120]{1,0:T(8,128)(2,1)}, bf16[64,5120]{1,0:T(8,128)(2,1)}, u32[]{:S(2)}, u32[]{:S(2)}) collective-permute-start(bf16[64,5120]{1,0:T(8,128)(2,1)} %pad_maximum_fusion.8), channel_id=1, source_target_pairs={{0,4},{2,6},{4,0},{6,2},{1,5},{3,7},{5,1},{7,3},{8,12},{10,14},{12... | collective-permute-start | bytes 1966088 | tf_op jit(solution)/shard_map/ppermute | solution.py:75
  190.1 35.2 %collective-permute-start.28 = (bf16[64,5120]{1,0:T(8,128)(2,1)}, bf16[64,5120]{1,0:T(8,128)(2,1)}, u32[]{:S(2)}, u32[]{:S(2)}) collective-permute-start(bf16[64,5120]{1,0:T(8,128)(2,1)} %pad_maximum_fusion.10), channel_id=1, source_target_pairs={{0,4},{2,6},{4,0},{6,2},{1,5},{3,7},{5,1},{7,3},{8,12},{10,14},{12... | collective-permute-start | bytes 1966088 | tf_op jit(solution)/shard_map/ppermute | solution.py:75
  195.6 107.5 %all-gather.8.cloned.1.call-start = ((), (), s32[]{:S(2)}) async-start(), calls=%async_computation.2 | async-start | bytes 3276800 | tf_op jit(solution)/shard_map/all_gather | solution.py:147
  202.2 24.3 %copy-start.22 = (f32[2,64,2560]{2,1,0:T(8,128)S(1)}, f32[2,64,2560]{2,1,0:T(8,128)}, u32[]{:S(2)}) copy-start(f32[2,64,2560]{2,1,0:T(8,128)} %copy-done.21) | copy-start | bytes 3932164
  203.5 23.0 %copy-start.20 = (f32[2,64,2560]{2,1,0:T(8,128)S(1)}, f32[2,64,2560]{2,1,0:T(8,128)}, u32[]{:S(2)}) copy-start(f32[2,64,2560]{2,1,0:T(8,128)} %copy-done.19) | copy-start | bytes 3932164
  227.0 16.9 %collective-permute-start.29 = (bf16[64,5120]{1,0:T(8,128)(2,1)S(1)}, bf16[64,5120]{1,0:T(8,128)(2,1)S(1)}, u32[]{:S(2)}, u32[]{:S(2)}) collective-permute-start(bf16[64,5120]{1,0:T(8,128)(2,1)S(1)} %pad_maximum_fusion.11), channel_id=1, source_target_pairs={{0,4},{2,6},{4,0},{6,2},{1,5},{3,7},{5,1},{7,3},{8,12},{10,14},{12... | collective-permute-start | bytes 1966088 | tf_op jit(solution)/shard_map/ppermute | solution.py:75
  244.2 10.3 %collective-permute-start.30 = (bf16[128,5120]{1,0:T(8,128)(2,1)S(1)}, bf16[128,5120]{1,0:T(8,128)(2,1)}, u32[]{:S(2)}, u32[]{:S(2)}) collective-permute-start(bf16[128,5120]{1,0:T(8,128)(2,1)S(1)} %pad_maximum_fusion.3), channel_id=1, source_target_pairs={{0,2},{2,0},{4,6},{6,4},{1,3},{3,1},{5,7},{7,5},{8,10},{10,8},{12,... | collective-permute-start | bytes 3932168 | tf_op jit(solution)/shard_map/ppermute | solution.py:70
  253.3 102.8 %collective-permute-start.6 = (bf16[128,2560]{1,0:T(8,128)(2,1)}, bf16[128,2560]{1,0:T(8,128)(2,1)S(1)}, u32[]{:S(2)}, u32[]{:S(2)}) collective-permute-start(bf16[128,2560]{1,0:T(8,128)(2,1)} %slice.169), channel_id=1, source_target_pairs={{0,1},{1,0},{2,3},{3,2},{4,5},{5,4},{6,7},{7,6},{8,9},{9,8},{10,11... | collective-permute-start | bytes 1966088 | tf_op jit(solution)/shard_map/ppermute | solution.py:67
  265.9 19.2 %collective-permute-start.31 = (bf16[128,2560]{1,0:T(8,128)(2,1)}, bf16[128,2560]{1,0:T(8,128)(2,1)}, u32[]{:S(2)}, u32[]{:S(2)}) collective-permute-start(bf16[128,2560]{1,0:T(8,128)(2,1)} %slice.166), channel_id=1, source_target_pairs={{0,1},{1,0},{2,3},{3,2},{4,5},{5,4},{6,7},{7,6},{8,9},{9,8},{10,11... | collective-permute-start | bytes 1966088 | tf_op jit(solution)/shard_map/ppermute | solution.py:67
  266.7 18.5 %copy-start.37 = (f32[256,2560]{1,0:T(8,128)S(1)}, f32[256,2560]{1,0:T(8,128)}, u32[]{:S(2)}) copy-start(f32[256,2560]{1,0:T(8,128)} %copy-done.36) | copy-start | bytes 7864324
  274.0 24.7 %collective-permute-start.15 = (bf16[128,2560]{1,0:T(8,128)(2,1)S(1)}, bf16[128,2560]{1,0:T(8,128)(2,1)S(1)}, u32[]{:S(2)}, u32[]{:S(2)}) collective-permute-start(bf16[128,2560]{1,0:T(8,128)(2,1)S(1)} %slice.168), channel_id=1, source_target_pairs={{0,1},{1,0},{2,3},{3,2},{4,5},{5,4},{6,7},{7,6},{8,9},{9,8},{10,11... | collective-permute-start | bytes 1966088 | tf_op jit(solution)/shard_map/ppermute | solution.py:67
  287.2 68.8 %collective-permute-start.32 = (bf16[128,2560]{1,0:T(8,128)(2,1)}, bf16[128,2560]{1,0:T(8,128)(2,1)}, u32[]{:S(2)}, u32[]{:S(2)}) collective-permute-start(bf16[128,2560]{1,0:T(8,128)(2,1)} %fusion), channel_id=1, source_target_pairs={{0,8},{8,16},{16,24},{24,0},{1,9},{9,17},{17,25},{25,1},{2,10},{10... | collective-permute-start | bytes 1966088 | tf_op jit(solution)/shard_map/ppermute | solution.py:67
  299.7 56.4 %collective-permute-start.16 = (bf16[128,2560]{1,0:T(8,128)(2,1)}, bf16[128,2560]{1,0:T(8,128)(2,1)}, u32[]{:S(2)}, u32[]{:S(2)}) collective-permute-start(bf16[128,2560]{1,0:T(8,128)(2,1)} %fusion.6), channel_id=1, source_target_pairs={{0,24},{8,0},{16,8},{24,16},{1,25},{9,1},{17,9},{25,17},{2,26},{10... | collective-permute-start | bytes 1966088 | tf_op jit(solution)/shard_map/ppermute | solution.py:67
  303.2 10.0 %copy-start.1 = (bf16[256,2560]{1,0:T(8,128)(2,1)S(1)}, bf16[256,2560]{1,0:T(8,128)(2,1)}, u32[]{:S(2)}) copy-start(bf16[256,2560]{1,0:T(8,128)(2,1)} %pad_maximum_fusion.2.refs_4_) | copy-start | bytes 3932164
  303.2 10.0 %copy-start.7 = (bf16[256,2560]{1,0:T(8,128)(2,1)S(1)}, bf16[256,2560]{1,0:T(8,128)(2,1)}, u32[]{:S(2)}) copy-start(bf16[256,2560]{1,0:T(8,128)(2,1)} %copy-done.6) | copy-start | bytes 3932164
  303.2 10.0 %copy-start.9 = (bf16[256,2560]{1,0:T(8,128)(2,1)S(1)}, bf16[256,2560]{1,0:T(8,128)(2,1)}, u32[]{:S(2)}) copy-start(bf16[256,2560]{1,0:T(8,128)(2,1)} %copy-done.8) | copy-start | bytes 3932164
  311.9 24.5 %collective-permute-start.22 = (bf16[128,2560]{1,0:T(8,128)(2,1)S(1)}, bf16[128,2560]{1,0:T(8,128)(2,1)S(1)}, u32[]{:S(2)}, u32[]{:S(2)}) collective-permute-start(bf16[128,2560]{1,0:T(8,128)(2,1)S(1)} %slice.167), channel_id=1, source_target_pairs={{0,1},{1,0},{2,3},{3,2},{4,5},{5,4},{6,7},{7,6},{8,9},{9,8},{10,11... | collective-permute-start | bytes 1966088 | tf_op jit(solution)/shard_map/ppermute | solution.py:67
  318.4 17.9 %copy-start.39 = (f32[256,2560]{1,0:T(8,128)S(1)}, f32[256,2560]{1,0:T(8,128)}, u32[]{:S(2)}) copy-start(f32[256,2560]{1,0:T(8,128)} %copy-done.38) | copy-start | bytes 7864324
  318.4 18.2 %copy-start.5 = (bf16[256,2560]{1,0:T(8,128)(2,1)S(1)}, bf16[256,2560]{1,0:T(8,128)(2,1)}, u32[]{:S(2)}) copy-start(bf16[256,2560]{1,0:T(8,128)(2,1)} %copy-done.4) | copy-start | bytes 3932164
  318.4 18.2 %copy-start.11 = (bf16[256,2560]{1,0:T(8,128)(2,1)S(1)}, bf16[256,2560]{1,0:T(8,128)(2,1)}, u32[]{:S(2)}) copy-start(bf16[256,2560]{1,0:T(8,128)(2,1)} %copy-done.10) | copy-start | bytes 3932164
  318.4 18.2 %copy-start.15 = (bf16[256,5120]{1,0:T(8,128)(2,1)S(1)}, bf16[256,5120]{1,0:T(8,128)(2,1)}, u32[]{:S(2)}) copy-start(bf16[256,5120]{1,0:T(8,128)(2,1)} %all-gather.4.cloned.1.call-done.refs_4_.refs_0_) | copy-start | bytes 7864324
  318.4 18.2 %copy-start.17 = (bf16[256,5120]{1,0:T(8,128)(2,1)S(1)}, bf16[256,5120]{1,0:T(8,128)(2,1)}, u32[]{:S(2)}) copy-start(bf16[256,5120]{1,0:T(8,128)(2,1)} %all-gather.6.cloned.1.call-done.refs_5_.refs_1_) | copy-start | bytes 7864324
  336.5 28.8 %copy-start.41 = (f32[256,2560]{1,0:T(8,128)S(1)}, f32[256,2560]{1,0:T(8,128)}, u32[]{:S(2)}) copy-start(f32[256,2560]{1,0:T(8,128)} %copy-done.40) | copy-start | bytes 7864324
  336.5 28.8 %collective-permute-start.23 = (bf16[128,2560]{1,0:T(8,128)(2,1)S(1)}, bf16[128,2560]{1,0:T(8,128)(2,1)S(1)}, u32[]{:S(2)}, u32[]{:S(2)}) collective-permute-start(bf16[128,2560]{1,0:T(8,128)(2,1)S(1)} %fusion.3), channel_id=1, source_target_pairs={{0,16},{8,24},{16,0},{24,8},{1,17},{9,25},{17,1},{25,9},{2,18},{10... | collective-permute-start | bytes 1966088 | tf_op jit(solution)/shard_map/ppermute | solution.py:67
  (31 other events, 107.9 us)
Sparse Core Ops, SparseCore 0:
  125.5 37.5 all-gather.3
  195.8 35.9 all-gather.5
  245.3 26.6 all-gather.7
